TPU v7x, 512 devices: a whole 4x8x8 slice. The times are simulated.
512 devices in a mesh: rows: 128 (over z, y, core), cols: 4 (over x).
Axes of the slice: x: 4, y: 8, z: 8, core: 2. Of those that a mesh axis runs over, the one named last changes fastest.
Arguments:
- points: bfloat16 [131072, 1024], P('rows', 'cols'), may hold values from -8 to 8
- factor: bfloat16 [131072, 1536], P('rows'), may hold values from -0.046875 to 0.046875
- targets: bfloat16 [131072, 512], P('rows', 'cols'), may hold values from -0.015625 to 0.015625
- pivot_slots: int32 [2, 1024], P(None, 'rows'), may hold values from 0 to 1023, as said below
- pivot_counts: int32 [2, 128], replicated, may hold values from 1 to 8, 256 in all within a row
Outputs:
- new_columns: float32 [2, 131072, 256], P(None, 'rows', 'cols')
- residual_diag: float32 [2, 131072], P(None, 'rows')
- coefficients: float32 [2, 256, 512], P(None, 'rows', 'cols')
Inputs may be any that keep to these rules, and one draw needn't show every extreme that they name: `pivot_slots`: within one index o of rows the 8 entries of each block, and those of the two blocks together, are distinct. `pivot_counts`: each block's counts sum to 256, and the largest count of each block is 8.
All inputs are finite; a program needn't handle non-finite values.
Results may differ from a plain program's by a relative error of at most 0.0058.
Values may be sent and summed in bfloat16 or wider, within the bound.
A program may use at most 64 MiB of HBM per device.

v0:
```python
import jax
import jax.numpy as jnp
from jax import lax
from jax.sharding import PartitionSpec as P

F = 1024
BLOCK = 256


def place_pivots(counts):
    inclusive = jnp.cumsum(counts)
    exclusive = inclusive - counts
    pick_index = jnp.arange(BLOCK, dtype=jnp.int32)
    owners = jnp.sum(
        (inclusive[None, :] <= pick_index[:, None]).astype(jnp.int32), axis=1, dtype=jnp.int32
    )
    owner_ids = jnp.arange(counts.shape[0], dtype=jnp.int32)
    starts = jnp.sum(
        jnp.where(owner_ids[None, :] == owners[:, None], exclusive[None, :], 0),
        axis=1,
        dtype=jnp.int32,
    )
    return (owners, pick_index - starts)


def cross_rows(left, right):
    return lax.dot_general(
        left, right, (((1,), (1,)), ((), ())), preferred_element_type=jnp.float32
    )


def low_inverse(block_dist, chosen_basis):
    pivot_block = jnp.exp(-block_dist / F) - cross_rows(chosen_basis, chosen_basis)
    cholesky_low = jnp.linalg.cholesky(pivot_block)
    identity = jnp.eye(pivot_block.shape[0], dtype=jnp.float32)
    return jax.scipy.linalg.solve_triangular(cholesky_low, identity, lower=True)


def solve_rows(columns, inverse):
    return lax.dot_general(
        columns,
        inverse,
        (((1,), (1,)), ((), ())),
        precision=lax.Precision.HIGHEST,
        preferred_element_type=jnp.float32,
    )


def local(points, factor, targets, pivot_slots, pivot_counts):
    col_index = lax.axis_index("cols")
    col_count = lax.axis_size("cols")
    slot_count = pivot_slots.shape[1]
    sq_part = jnp.sum(jnp.square(points.astype(jnp.float32)), axis=1)
    current = factor
    residual = 1.0 - jnp.sum(jnp.square(factor.astype(jnp.float32)), axis=1)
    outputs_new = []
    outputs_res = []
    outputs_coeff = []
    for section_index in range(2):
        owners, slot_pos = place_pivots(pivot_counts[section_index])
        places = owners * slot_count + slot_pos
        slot_points = jnp.take(points, pivot_slots[section_index], axis=0)
        slot_basis = jnp.take(current, pivot_slots[section_index], axis=0)
        gathered_points, gathered_basis = (
            lax.all_gather(slot_points, "rows", axis=0, tiled=True),
            lax.all_gather(slot_basis, "rows", axis=0, tiled=True),
        )
        chosen = jnp.take(gathered_points, places, axis=0)
        chosen_basis = jnp.take(gathered_basis, places, axis=0)
        pivot_sq = jnp.sum(jnp.square(chosen.astype(jnp.float32)), axis=1)
        dist_part = sq_part[:, None] + pivot_sq[None, :] - 2.0 * cross_rows(points, chosen)
        block_part = pivot_sq[:, None] + pivot_sq[None, :] - 2.0 * cross_rows(chosen, chosen)
        distance, block_dist = lax.psum((dist_part, block_part), "cols")
        inverse = low_inverse(block_dist, chosen_basis)
        columns = jnp.exp(-distance / F) - cross_rows(current, chosen_basis)
        fresh_cols = solve_rows(columns, inverse)
        narrow = fresh_cols.astype(jnp.bfloat16)
        residual = residual - jnp.sum(jnp.square(fresh_cols), axis=1)
        coeff_part = lax.dot_general(
            narrow, targets, (((0,), (0,)), ((), ())), preferred_element_type=jnp.float32
        )
        outputs_coeff.append(lax.psum_scatter(coeff_part, "rows", scatter_dimension=0, tiled=True))
        part_width = fresh_cols.shape[1] // col_count
        outputs_new.append(
            lax.dynamic_slice_in_dim(fresh_cols, col_index * part_width, part_width, 1)
        )
        outputs_res.append(residual)
        current = jnp.concatenate([current, narrow], axis=1)
    stacked = jnp.stack(outputs_coeff, axis=0)
    return (jnp.stack(outputs_new, axis=0), jnp.stack(outputs_res, axis=0), stacked)


def solution(mesh):
    in_specs = (P("rows", "cols"), P("rows", None), P("rows", "cols"), P(None, "rows"), P())
    out_specs = (P(None, "rows", "cols"), P(None, "rows"), P(None, "rows", "cols"))
    return jax.shard_map(local, mesh=mesh, in_specs=in_specs, out_specs=out_specs, check_vma=False)
```

profile of v0, /device:TPU:1, one launch (start us, length us, event | category | flops | bytes accessed | tf_op | source)
XLA Modules:
  0.0 671.6 jit_solution(12107818943278220246)
XLA Ops:
  9.6 2.9 gather_fusion
  13.3 1.7 gather_fusion.4
  15.0 1.7 gather_fusion.6
  19.4 59.0 %all_gather.14 = bf16[1024,256]{1,0:T(8,128)(2,1)S(1)} all-gather(bf16[8,256]{1,0:T(8,128)(2,1)S(1)} %broadcast_select_fusion.10), channel_id=1, replica_groups=mesh['rows'=128,'cols'=4] {'rows'}, dimensions={0}, use_global_device_ids=true | all-gather | bytes 528384 | tf_op jit(solution)/shard_map/all_gather | solution.py:65
  78.3 1.2 gather_fusion.7
  79.9 48.8 %all_gather.12 = bf16[1024,256]{1,0:T(8,128)(2,1)S(1)} all-gather(bf16[8,256]{1,0:T(8,128)(2,1)S(1)} %broadcast_select_fusion.11), channel_id=1, replica_groups=mesh['rows'=128,'cols'=4] {'rows'}, dimensions={0}, use_global_device_ids=true | all-gather | bytes 528384 | tf_op jit(solution)/shard_map/all_gather | solution.py:65
  128.7 1.2 gather_fusion.5
  130.5 1.0 fusion.5
  131.5 1.0 fusion.6
  132.5 1.3 fusion.3
  133.8 1.3 fusion.1
  136.9 5.4 gather_fusion.1
  142.3 66.0 %all-reduce.10.cloned.1.call-done = (f32[1024,256]{0,1:T(8,128)}, f32[1024,256]{0,1:T(8,128)}, f32[256,256]{0,1:T(8,128)}, f32[256,256]{0,1:T(8,128)}) async-done(((f32[1024,256]{0,1:T(8,128)}, f32[1024,256]{0,1:T(8,128)}, f32[256,256]{0,1:T(8,128)}, f32[256,256]{0,1:T(8,128)}), (f32[1024,256]{0,1:T(8,128)}, f32[1024,256]{0,1:T(8,128)}, f32[256,256]{0,1:T(8,128)}, ...) | async-done | bytes 2621456 | tf_op jit(solution)/shard_map/psum | solution.py:73
  208.3 2.8 convolution_subtract_fusion.2
  211.1 3.5 fusion.4
  214.6 1.8 copy.39
  216.4 1.1 fusion.18
  218.2 11.7 %cholesky.130 = f32[128,128]{1,0:T(8,128)S(1)} custom-call(f32[128,128]{1,0:T(8,128)S(1)} %cholesky.194), custom_call_target="Cholesky" | custom-call | tf_op jit(solution)/shard_map/jit(cholesky)/cholesky | solution.py:34
  230.6 10.4 %custom-call.13 = f32[1,128,128]{1,2,0:T(8,128)} custom-call(f32[1,128,128]{2,1,0:T(8,128)S(1)} %get-tuple-element.66), custom_call_target="InvertDiagBlocksLowerTriangular" | custom-call | tf_op jit(solution)/shard_map/jit(cholesky)/cholesky | solution.py:34
  241.7 1.7 constant_dynamic-update-slice_fusion.3
  243.4 1.1 convolution_subtract_fusion.6
  244.5 24.6 %cholesky.147 = f32[128,128]{1,0:T(8,128)S(1)} custom-call(f32[128,128]{1,0:T(8,128)S(1)} %convolution_subtract_fusion.6), custom_call_target="Cholesky" | custom-call | tf_op jit(solution)/shard_map/jit(cholesky)/cholesky | solution.py:34
  271.8 1.7 select_select_fusion.1
  273.5 1.3 triangular_solve.75
  274.8 7.2 %while.4 = (s32[]{:T(128)}, f32[256,256]{1,0:T(8,128)}, s32[2,2]{1,0:T(2,128)}, f32[2,128,128]{2,1,0:T(8,128)S(1)}, s32[]{:T(128)}) while((s32[]{:T(128)}, f32[256,256]{1,0:T(8,128)}, s32[2,2]{1,0:T(2,128)}, f32[2,128,128]{2,1,0:T(8,128)S(1)}, s32[]{:T(128)}) %tuple.62), condition=%wide.while_cond, body=%wide.while_body.sunk | while | flops 2 | bytes 131189 | solution.py:36
  276.1 2.3 bitcast_dynamic-update-slice_fusion.4
  279.8 2.2 bitcast_dynamic-update-slice_fusion.4
  282.6 20.5 %custom-call.14 = f32[2,128,128]{1,2,0:T(8,128)S(1)} custom-call(f32[2,128,128]{2,1,0:T(8,128)} %copy-done.9), custom_call_target="InvertDiagBlocksLowerTriangular" | custom-call | tf_op jit(solution)/shard_map/jit(_solve_triangular)/triangular_solve | solution.py:36
  303.1 1.2 fusion.22
  304.3 1.2 convolution_subtract_fusion.4
  305.9 3.5 multiply_reduce_fusion.2
  309.3 2.1 copy.41
  311.4 3.1 pad_maximum_fusion
  314.5 3.1 gather_fusion.2
  318.3 1.3 dynamic-slice.5
  320.9 1.7 dynamic-slice_bitcast_fusion.1
  323.5 79.6 %all-gather.5.cloned.1.call-done = bf16[1024,1792]{1,0:T(8,128)(2,1)} async-done(((bf16[8,1792]{1,0:T(8,128)(2,1)}), bf16[1024,1792]{1,0:T(8,128)(2,1)}) %all-gather.5.cloned.1.call-update) | async-done | bytes 3670032 | tf_op jit(solution)/shard_map/all_gather | solution.py:66
  403.2 5.6 gather_fusion.3
  408.8 3.9 convolution_subtract_fusion
  413.4 11.7 %cholesky.164 = f32[128,128]{1,0:T(8,128)S(1)} custom-call(f32[128,128]{1,0:T(8,128)S(1)} %cholesky.197), custom_call_target="Cholesky" | custom-call | tf_op jit(solution)/shard_map/jit(cholesky)/cholesky | solution.py:34
  425.8 9.8 %custom-call.15 = f32[1,128,128]{1,2,0:T(8,128)S(1)} custom-call(f32[1,128,128]{2,1,0:T(8,128)S(1)} %get-tuple-element.62), custom_call_target="InvertDiagBlocksLowerTriangular" | custom-call | tf_op jit(solution)/shard_map/jit(cholesky)/cholesky | solution.py:34
  436.1 11.9 %cholesky.181 = f32[128,128]{1,0:T(8,128)S(1)} custom-call(f32[128,128]{1,0:T(8,128)S(1)} %convolution_subtract_fusion.5), custom_call_target="Cholesky" | custom-call | tf_op jit(solution)/shard_map/jit(cholesky)/cholesky | solution.py:34
  450.2 4.0 while.5
  450.8 1.4 bitcast_dynamic-update-slice_fusion.5
  452.8 1.4 bitcast_dynamic-update-slice_fusion.5
  454.2 19.7 %custom-call.16 = f32[2,128,128]{1,2,0:T(8,128)S(1)} custom-call(f32[2,128,128]{2,1,0:T(8,128)S(1)} %get-tuple-element.22), custom_call_target="InvertDiagBlocksLowerTriangular" | custom-call | tf_op jit(solution)/shard_map/jit(_solve_triangular)/triangular_solve | solution.py:36
  474.8 1.1 multiply_reduce_fusion.1
  478.3 183.9 %all-reduce.8.cloned.1.call-done = (f32[256,128]{1,0:T(8,128)}, f32[256,128]{1,0:T(8,128)}) async-done(((f32[256,128]{1,0:T(8,128)}, f32[256,128]{1,0:T(8,128)}), (f32[256,128]{1,0:T(8,128)}, f32[256,128]{1,0:T(8,128)})) %all-reduce.8.cloned.1.call-update) | async-done | bytes 262160
  (111 shorter events, 26.4 us)
Async XLA Ops:
  8.0 314.6 %copy-start = (bf16[1024,128]{1,0:T(8,128)(2,1)S(1)}, bf16[1024,128]{1,0:T(8,128)(2,1)}, u32[]{:S(2)}) copy-start(bf16[1024,128]{1,0:T(8,128)(2,1)} %param.14) | copy-start | bytes 786436
  8.0 122.2 %copy-start.2 = (bf16[1024,256]{1,0:T(8,128)(2,1)S(1)}, bf16[1024,256]{1,0:T(8,128)(2,1)}, u32[]{:S(2)}) copy-start(bf16[1024,256]{1,0:T(8,128)(2,1)} %param.12) | copy-start | bytes 1572868
  8.0 128.9 %all-gather.3.cloned.1.call-start = ((), (), s32[]{:S(2)}) async-start(), calls=%async_computation | async-start | bytes 3170304 | tf_op jit(solution)/shard_map/all_gather | solution.py:66
  13.2 195.1 %all-reduce.10.cloned.1.call-start = ((), (), s32[]{:S(2)}) async-start(), calls=%async_computation.3 | async-start | bytes 5242880 | tf_op jit(solution)/shard_map/psum | solution.py:73
  135.2 268.0 %all-gather.5.cloned.1.call-start = ((), (), s32[]{:S(2)}) async-start(), calls=%async_computation.1 | async-start | bytes 3698688 | tf_op jit(solution)/shard_map/all_gather | solution.py:66
  136.9 74.2 %copy-start.1 = (bf16[1024,1536]{1,0:T(8,128)(2,1)S(1)}, bf16[1024,1536]{1,0:T(8,128)(2,1)}, u32[]{:S(2)}) copy-start(bf16[1024,1536]{1,0:T(8,128)(2,1)} %param.13) | copy-start | bytes 9437188
  217.4 0.7 copy-start.8
  282.0 0.6 copy-start.9
  318.3 344.0 %all-reduce.8.cloned.1.call-start = ((), (), s32[]{:S(2)}) async-start(), calls=%async_computation.2 | async-start | bytes 524288
  320.2 2.4 copy-start.3
  408.8 3.9 copy-start.7
  408.8 3.9 copy-start.10
  412.7 37.5 %copy-start.11 = (s32[2,2]{1,0:T(2,128)S(1)}, s32[2,2]{1,0:T(2,128)}, u32[]{:S(2)}) copy-start(s32[2,2]{1,0:T(2,128)} %get-tuple-element.212) | copy-start | bytes 52
  412.7 61.2 %copy-start.4 = (f32[256,256]{1,0:T(8,128)S(1)}, f32[256,256]{1,0:T(8,128)}, u32[]{:S(2)}) copy-start(f32[256,256]{1,0:T(8,128)} %fusion.19) | copy-start | bytes 786436
  412.7 62.1 %copy-start.5 = (f32[1024,256]{0,1:T(8,128)S(1)}, f32[1024,256]{0,1:T(8,128)}, u32[]{:S(2)}) copy-start(f32[1024,256]{0,1:T(8,128)} %convolution_subtract_fusion) | copy-start | bytes 3145732
  448.0 29.5 %copy-start.6 = (f32[1,1024,64]{1,2,0:T(8,128)S(1)}, f32[1,1024,64]{1,2,0:T(8,128)}, u32[]{:S(2)}) copy-start(f32[1,1024,64]{1,2,0:T(8,128)} %dynamic-slice_bitcast_fusion.1) | copy-start | bytes 786436
Sparse Core Ops, SparseCore 0:
  13.3 89.6 all-gather.2
  318.4 84.7 all-gather.4
  477.0 185.2 all-reduce.7
Sparse Core Ops, SparseCore 1:
  135.2 73.0 all-reduce.9
where the time goes:
time: 674 us; the launch traced here: 672 us
  waiting for transfers between devices  330 us (49%)
  other arithmetic  139 us (21%)
  blocking collectives  108 us (16%)
  local copies, waits for them, and re-layouts  46.5 us (7%)
  matrix products  28.7 us (4%)
  between operations  19.1 us (3%)
    unnamed x5, waiting for transfers between devices  184 us
    all_gather x2, blocking collectives, local(): lax.all_gather(slot_points, 'rows', axis=0, tiled=True)  108 us
    another operation x14, other arithmetic, low_inverse(): cholesky_low = jnp.linalg.cholesky(pivot_block)  83.6 us
    all_gather x2, waiting for transfers between devices, local(): lax.all_gather(slot_basis, 'rows', axis=0, tiled=True)  79.6 us
    psum x1, waiting for transfers between devices, local(): distance, block_dist = lax.psum((dist_part, block_part), 'cols')  66 us
    another operation x5, other arithmetic, low_inverse(): return jax.scipy.linalg.solve_triangular(cholesky_low, identity, lower=True)  42.4 us
    dot_general x8, matrix products, cross_rows(): lax.dot_general(left, right, (((1,), (1,)), ((), ())), preferred_element_...  15.4 us
  transfers between devices with their start and end apart: 4, of which 3 were waited for; matrix products, arithmetic and copies ran while one was open for 4% of the time, Pallas kernels for 0%

commit v1 on v0

v1 whole, which is shorter than its diff:
```python
import functools
import jax
import jax.numpy as jnp
from jax import lax
from jax.experimental import pallas as pl
from jax.experimental.pallas import tpu as pltpu
from jax.sharding import PartitionSpec as P

F = 1024
BLOCK = 256
MAXP = 8
NX = 4
FQ = 256
KQ = 384
W = FQ + KQ
ROWS = 1024
TILE = 256
HI = lax.Precision.HIGHEST
f32 = jnp.float32
bf16 = jnp.bfloat16


def mm_nt(a, b, precision=None):
    return lax.dot_general(
        a, b, (((1,), (1,)), ((), ())), precision=precision, preferred_element_type=f32
    )


def mm_nn(a, b, precision=None):
    return lax.dot_general(
        a, b, (((1,), (0,)), ((), ())), precision=precision, preferred_element_type=f32
    )


def mm_tn(a, b):
    return lax.dot_general(a, b, (((0,), (0,)), ((), ())), preferred_element_type=f32)


def split2(a):
    high = a.astype(bf16)
    return high, (a - high.astype(f32)).astype(bf16)


def chol_inv_128(a):
    n = 16
    sub = lax.broadcasted_iota(jnp.int32, (8, 128), 0)
    lane = lax.broadcasted_iota(jnp.int32, (8, 128), 1)
    A = [a[8 * r : 8 * r + 8, :] for r in range(n)]
    X = [jnp.where(lane == sub + 8 * r, 1.0, 0.0).astype(f32) for r in range(n)]
    out = []
    for k in range(n):
        panel = [
            [jnp.broadcast_to(A[r][:, 8 * k + m : 8 * k + m + 1], (8, 128)) for m in range(8)]
            if r >= k
            else None
            for r in range(n)
        ]
        pivots = jnp.ones((8, 128), f32)
        for j in range(8):
            row = lambda v: jnp.broadcast_to(v[j : j + 1, :], (8, 128))
            row_a, row_x = row(A[k]), row(X[k])
            row_p = [row(panel[k][m]) if m >= j else None for m in range(8)]
            pivots = jnp.where(sub == j, row_p[j], pivots)
            inverse = 1.0 / row_p[j]
            for r in range(k, n):
                c = panel[r][j] * inverse
                if r == k:
                    if j == 7:
                        continue
                    c = jnp.where(sub > j, c, 0.0)
                A[r] = A[r] - c * row_a
                X[r] = X[r] - c * row_x
                for m in range(j + 1, 8):
                    panel[r][m] = panel[r][m] - c * row_p[m]
        out.append(X[k] * lax.rsqrt(pivots))
    return jnp.concatenate(out, axis=0)


def chol_inv_256(a):
    inv11 = chol_inv_128(a[:128, :128])
    low21 = mm_nt(a[128:, :128], inv11, HI)
    inv22 = chol_inv_128(a[128:, 128:] - mm_nt(low21, low21, HI))
    inv21 = -mm_nn(inv22, mm_nn(low21, inv11, HI), HI)
    zero = jnp.zeros((128, 128), f32)
    return jnp.concatenate(
        [jnp.concatenate([inv11, zero], axis=1), jnp.concatenate([inv21, inv22], axis=1)], axis=0
    )


def factor_kernel(g_ref, inv_ref, cross_ref, sq_ref):
    def gram(a, b):
        ra, rb = slice(256 * a, 256 * a + 256), slice(256 * b, 256 * b + 256)
        dots = sum(mm_nt(g_ref[c, ra, :FQ], g_ref[c, rb, :FQ]) for c in range(NX))
        basis = sum(mm_nt(g_ref[c, ra, FQ:], g_ref[c, rb, FQ:]) for c in range(NX))
        return dots, basis

    eye = lax.broadcasted_iota(jnp.int32, (256, 256), 0) == lax.broadcasted_iota(
        jnp.int32, (256, 256), 1
    )

    def norms(dots):
        diag = jnp.where(eye, dots, 0.0)
        return jnp.sum(diag, axis=1, keepdims=True), jnp.sum(diag, axis=0, keepdims=True)

    dots00, basis00 = gram(0, 0)
    dots10, basis10 = gram(1, 0)
    dots11, basis11 = gram(1, 1)
    col0, row0 = norms(dots00)
    col1, row1 = norms(dots11)
    sq_ref[:, :256] = jnp.broadcast_to(row0, (8, 256))
    sq_ref[:, 256:] = jnp.broadcast_to(row1, (8, 256))
    a00 = jnp.exp(-(col0 + row0 - 2.0 * dots00) / F) - basis00
    a10 = jnp.exp(-(col1 + row0 - 2.0 * dots10) / F) - basis10
    a11 = jnp.exp(-(col1 + row1 - 2.0 * dots11) / F) - basis11
    inv0 = chol_inv_256(a00)
    narrow10 = mm_nt(a10, inv0, HI).astype(bf16)
    inv1 = chol_inv_256(a11 - mm_nt(narrow10, narrow10))
    cross_ref[...] = narrow10
    inv_ref[0, 0], inv_ref[0, 1] = split2(inv0)
    inv_ref[1, 0], inv_ref[1, 1] = split2(inv1)


def factor_pivots(g):
    return pl.pallas_call(
        factor_kernel,
        out_shape=(
            jax.ShapeDtypeStruct((2, 2, BLOCK, BLOCK), bf16),
            jax.ShapeDtypeStruct((BLOCK, BLOCK), bf16),
            jax.ShapeDtypeStruct((8, 2 * BLOCK), f32),
        ),
        compiler_params=pltpu.CompilerParams(vmem_limit_bytes=40 * 2**20),
        cost_estimate=pl.CostEstimate(
            flops=60_000_000_000, bytes_accessed=4_000_000, transcendentals=0
        ),
        name="pivot_factor",
    )(g)


def fold(v):
    total = v[:, :128]
    for i in range(1, v.shape[1] // 128):
        total = total + v[:, 128 * i : 128 * i + 128]
    return total


def rows_kernel(place_ref, x_ref, f_ref, t_ref, g_ref, inv_ref, cross_ref, sq_ref, new_ref, res_ref, coef_ref):
    place = place_ref[0]
    dots = jnp.zeros((TILE, 512), f32)
    basis = jnp.zeros((TILE, 512), f32)
    squares = jnp.zeros((TILE, 128), f32)
    factor_squares = jnp.zeros((TILE, 128), f32)
    for c in range(NX):
        x = x_ref[c]
        fac = f_ref[:, KQ * c : KQ * c + KQ]
        dots = dots + mm_nt(x, g_ref[c, :, :FQ])
        basis = basis + mm_nt(fac, g_ref[c, :, FQ:])
        squares = squares + fold(jnp.square(x.astype(f32)))
        factor_squares = factor_squares + fold(jnp.square(fac.astype(f32)))
    sq = jnp.sum(squares, axis=1, keepdims=True)
    columns = jnp.exp(-(sq + sq_ref[0:1, :] - 2.0 * dots) / F) - basis

    def solve(b, cols):
        high, low = split2(cols)
        return (
            mm_nt(high, inv_ref[b, 0]) + mm_nt(high, inv_ref[b, 1]) + mm_nt(low, inv_ref[b, 0])
        )

    def keep(b, fresh):
        half = jnp.where(place >= 2, fresh[:, 128:], fresh[:, :128])
        part = jnp.where(place % 2 == 1, pltpu.roll(half, 64, 1), half)
        new_ref[b] = part[:, :64]

    def across(v):
        return jnp.sum(jnp.transpose(v), axis=0, keepdims=True)

    @pl.when(pl.program_id(0) == 0)
    def _():
        coef_ref[...] = jnp.zeros_like(coef_ref)

    fresh0 = solve(0, columns[:, :256])
    narrow0 = fresh0.astype(bf16)
    fresh1 = solve(1, columns[:, 256:] - mm_nt(narrow0, cross_ref[...]))
    narrow1 = fresh1.astype(bf16)
    keep(0, fresh0)
    keep(1, fresh1)
    res0 = 1.0 - across(factor_squares + fold(jnp.square(fresh0)))
    res_ref[0:1, :] = res0
    res_ref[1:2, :] = res0 - across(fold(jnp.square(fresh1)))
    coef_ref[:256] += mm_tn(narrow0, t_ref[...])
    coef_ref[256:] += mm_tn(narrow1, t_ref[...])


def solve_rows(place, x, factor, targets, g, inv, cross, sq):
    whole = lambda shape: pl.BlockSpec(shape, lambda i: (0,) * len(shape))
    return pl.pallas_call(
        rows_kernel,
        grid=(ROWS // TILE,),
        in_specs=[
            pl.BlockSpec(memory_space=pltpu.SMEM),
            pl.BlockSpec((NX, TILE, FQ), lambda i: (0, i, 0)),
            pl.BlockSpec((TILE, NX * KQ), lambda i: (i, 0)),
            pl.BlockSpec((TILE, 128), lambda i: (i, 0)),
            whole((NX, 512, W)),
            whole((2, 2, BLOCK, BLOCK)),
            whole((BLOCK, BLOCK)),
            whole((8, 512)),
        ],
        out_specs=[
            pl.BlockSpec((2, TILE, 64), lambda i: (0, i, 0)),
            pl.BlockSpec((2, TILE), lambda i: (0, i)),
            whole((512, 128)),
        ],
        out_shape=(
            jax.ShapeDtypeStruct((2, ROWS, 64), f32),
            jax.ShapeDtypeStruct((2, ROWS), f32),
            jax.ShapeDtypeStruct((512, 128), f32),
        ),
        compiler_params=pltpu.CompilerParams(vmem_limit_bytes=40 * 2**20),
        name="row_solve",
    )(place, x, factor, targets, g, inv, cross, sq)


def place_pivots(counts):
    inclusive = jnp.cumsum(counts)
    exclusive = inclusive - counts
    pick_index = jnp.arange(BLOCK, dtype=jnp.int32)
    owners = jnp.sum(
        (inclusive[None, :] <= pick_index[:, None]).astype(jnp.int32), axis=1, dtype=jnp.int32
    )
    owner_ids = jnp.arange(counts.shape[0], dtype=jnp.int32)
    starts = jnp.sum(
        jnp.where(owner_ids[None, :] == owners[:, None], exclusive[None, :], 0),
        axis=1,
        dtype=jnp.int32,
    )
    return owners, pick_index - starts


def local(points, factor, targets, pivot_slots, pivot_counts):
    place = lax.axis_index("cols")
    quarter = lax.dynamic_slice_in_dim(factor, place * KQ, KQ, 1)
    rows = pivot_slots.reshape(2 * MAXP)
    slots = jnp.concatenate([points[rows], quarter[rows]], axis=1)
    gathered = lax.all_gather(slots, "rows", axis=0, tiled=False)
    picks = []
    for b in range(2):
        owners, slot = place_pivots(pivot_counts[b])
        picks.append(owners * 2 * MAXP + b * MAXP + slot)
    chosen = jnp.take(gathered.reshape(-1, W), jnp.concatenate(picks), axis=0)
    g = lax.all_gather(chosen, "cols", axis=0, tiled=False)
    x = lax.all_gather(points, "cols", axis=0, tiled=False)
    inv, cross, sq = factor_pivots(g)
    new, res, coef = solve_rows(
        place.reshape(1).astype(jnp.int32), x, factor, targets, g, inv, cross, sq
    )
    coef = lax.psum_scatter(
        coef.reshape(2, BLOCK, 128), "rows", scatter_dimension=1, tiled=True
    )
    return new, res, coef


def solution(mesh):
    in_specs = (P("rows", "cols"), P("rows", None), P("rows", "cols"), P(None, "rows"), P())
    out_specs = (P(None, "rows", "cols"), P(None, "rows"), P(None, "rows", "cols"))
    return jax.shard_map(local, mesh=mesh, in_specs=in_specs, out_specs=out_specs, check_vma=False)
```

time: 674 us -> 396 us (0.59)
  other arithmetic: 139 us -> 3.46 us
  blocking collectives: 108 us -> 0 us
  Pallas kernels: 0 us -> 29.2 us
  matrix products: 28.7 us -> 0 us
  local copies, waits for them, and re-layouts: 46.5 us -> 23 us
    another operation x26 -> x4, other arithmetic: 129 us -> 0.55 us  [the longest x14 83.6 us: low_inverse(): cholesky_low = jnp.linalg.cholesky(pivot_block)]
    all_gather x2 -> x0, blocking collectives: 108 us -> none  [local(): lax.all_gather(slot_points, 'rows', axis=0, tiled=True)]
    psum x1 -> x0, waiting for transfers between devices: 66 us -> none  [local(): distance, block_dist = lax.psum((dist_part, block_part), 'cols')]
    all_gather x2 -> x3, waiting for transfers between devices: 79.6 us -> 139 us  [the longest x1 86.7 us: local(): gathered = lax.all_gather(slots, 'rows', axis=0, tiled=False)]
    pallas_call x0 -> x2, Pallas kernels: none -> 29.2 us  [the longest x1 20.2 us: factor_pivots(): pl.pallas_call(factor_kernel, out_shape=(jax.ShapeDtypeStruct((2, 2, BLOC...]
    dot_general x12 -> x0, matrix products: 21.9 us -> none  [the longest x8 15.4 us: cross_rows(): lax.dot_general(left, right, (((1,), (1,)), ((), ())), preferred_element_...]
    another operation x26 -> x1, local copies, waits for them, and re-layouts: 17.2 us -> 0.11 us  [the longest x15 12.4 us: low_inverse(): return jax.scipy.linalg.solve_triangular(cholesky_low, identity, lower=True)]
    gather x8 -> x3, local copies, waits for them, and re-layouts: 22.6 us -> 6.49 us  [the longest x1 4.21 us: local(): chosen = jnp.take(gathered.reshape(-1, W), jnp.concatenate(picks), axis=0)]
  transfers between devices with their start and end apart: 4 -> 4, of which waited for: 3 -> 4; matrix products, arithmetic and copies ran while one was open for 4% -> 2% of each run, Pallas kernels for 0% -> 5%
where the time goes in v1:
time: 396 us; the launch traced here: 395 us
  waiting for transfers between devices  324 us (82%)
  Pallas kernels  29.2 us (7%)
  local copies, waits for them, and re-layouts  23 us (6%)
  between operations  14.5 us (4%)
    unnamed x5, waiting for transfers between devices  185 us
    all_gather x1, waiting for transfers between devices, local(): gathered = lax.all_gather(slots, 'rows', axis=0, tiled=False)  86.7 us
    all_gather x1, waiting for transfers between devices, local(): g = lax.all_gather(chosen, 'cols', axis=0, tiled=False)  36.1 us
    pallas_call x1, Pallas kernels, factor_pivots(): pl.pallas_call(factor_kernel, out_shape=(jax.ShapeDtypeStruct((2, 2, BLOC...  20.2 us
    all_gather x1, waiting for transfers between devices, local(): x = lax.all_gather(points, 'cols', axis=0, tiled=False)  15.8 us
    unnamed x21, local copies, waits for them, and re-layouts  13.5 us
    pallas_call x1, Pallas kernels, solve_rows(): pl.pallas_call(rows_kernel, grid=(ROWS // TILE,), in_specs=[pl.BlockSpec(...  9.08 us
  transfers between devices with their start and end apart: 4, of which 4 were waited for; matrix products, arithmetic and copies ran while one was open for 2% of the time, Pallas kernels for 5%

profile of v1, /device:TPU:1, one launch (start us, length us, event | category | flops | bytes accessed | tf_op | source)
XLA Modules:
  0.0 394.6 jit_solution(303065934927323498)
XLA Ops:
  7.2 0.0 all-gather.10.cloned.1.call-start
  7.2 0.8 reshape.171
  8.0 1.2 constant_dynamic-slice_fusion.1
  9.2 0.6 gather_fusion.1
  9.8 1.7 gather_fusion
  11.5 0.6 pad_maximum_fusion
  12.1 0.0 all-gather.10.cloned.1.call-update
  12.1 0.0 all-gather.6.cloned.1.call-start
  12.2 0.8 slice_bitcast_fusion.1
  12.9 0.1 copy.17
  13.1 0.2 reduce-window.6
  13.2 0.1 reduce
  13.3 0.1 copy.18
  13.4 0.2 reduce-window.9
  13.6 0.1 reduce.2
  13.7 0.1 convert_reduce_fusion
  13.9 0.1 convert_reduce_fusion.1
  14.0 0.8 fusion.2
  14.7 0.2 select_reduce_fusion
  15.1 86.7 %all-gather.10.cloned.1.call-done = bf16[2048,640]{1,0:T(8,128)(2,1)} async-done(((bf16[16,640]{1,0:T(8,128)(2,1)}), bf16[2048,640]{1,0:T(8,128)(2,1)}) %all-gather.10.cloned.1.call-update) | async-done | bytes 2621456 | tf_op jit(solution)/shard_map/all_gather | solution.py:244
  101.8 4.2 %gather_fusion.2 = bf16[512,640]{1,0:T(8,128)(2,1)S(1)} fusion(bf16[2048,640]{1,0:T(8,128)(2,1)} %all-gather.10.cloned.1.call-done, s32[1024]{0:T(1024)S(1)} %pad_clamp_fusion), kind=kCustom, calls=%fused_computation.2 | custom fusion | bytes 1312768 | tf_op jit(solution)/shard_map/jit(_take)/gather | solution.py:249
  106.0 1.0 bitcast_select_fusion
  107.0 0.0 all-gather.6.cloned.1.call-update
  107.0 0.0 all-gather.8.cloned.1.call-start
  107.1 0.0 copy-start.7
  107.1 0.7 all-gather.8.cloned.1.call-update
  107.7 0.0 copy-start
  107.8 0.2 all-reduce.3.cloned.1.call-start
  108.0 36.1 %all-gather.6.cloned.1.call-done.g_ref = bf16[4,512,640]{2,1,0:T(8,128)(2,1)} async-done(((bf16[1,512,640]{2,1,0:T(8,128)(2,1)}), bf16[4,512,640]{2,1,0:T(8,128)(2,1)}) %all-gather.6.cloned.1.call-update) | async-done | bytes 2621456 | tf_op jit(solution)/shard_map/all_gather | solution.py:250
  144.1 0.0 copy-start.1
  144.1 1.7 copy-done.1
  145.8 20.2 %pivot_factor.1 = (bf16[2,2,256,256]{3,2,1,0:T(8,128)(2,1)S(1)}, bf16[256,256]{1,0:T(8,128)(2,1)S(1)}, f32[8,512]{1,0:T(8,128)S(1)}) custom-call(bf16[4,512,640]{2,1,0:T(8,128)(2,1)S(1)} %copy-done.1), custom_call_target="tpu_custom_call" | custom-call | flops 60000002048 | bytes 4000000 | tf_op jit(solution)/shard_map/pivot_factor/pallas_call | solution.py:124
  166.0 0.0 copy-start.5
  166.0 0.8 copy-done.5
  166.8 15.8 %all-gather.8.cloned.1.call-done = bf16[4096,256]{1,0:T(8,128)(2,1)} async-done(((bf16[1024,256]{1,0:T(8,128)(2,1)}), bf16[4096,256]{1,0:T(8,128)(2,1)}) %all-gather.8.cloned.1.call-update) | async-done | bytes 2097168 | tf_op jit(solution)/shard_map/all_gather | solution.py:251
  182.5 0.0 copy-done.7
  182.5 0.0 copy-done
  182.6 1.7 copy-done.2
  184.3 1.6 copy-done.3
  185.9 1.0 copy-done.6
  186.9 9.1 %row_solve.1 = (f32[2,1024,64]{2,1,0:T(8,128)S(1)}, f32[2,1024]{1,0:T(2,128)}, f32[512,128]{1,0:T(8,128)S(1)}) custom-call(s32[1]{0:T(128)} %bitcast.2.place_ref, bf16[4,1024,256]{2,1,0:T(8,128)(2,1)S(1)} %bitcast.29, bf16[1024,1536]{1,0:T(8,128)(2,1)S(1)} %copy-done, bf16[1024,128]{1,0:T(8,128)(2,1)S(1)} %copy-done.7, bf16[4,512,640]{2,1,0:T(8,128)(2,1)S(1)} %copy-done.2, ...), custom_call_target="tpu_custom_call" | custom-call | tf_op jit(solution)/shard_map/row_solve/pallas_call | solution.py:195
  196.0 1.0 copy-done.4
  197.0 0.7 copy-done.8
  197.7 0.0 all-reduce.3.cloned.1.call-update
  197.7 1.3 dynamic-slice
  199.7 2.3 copy.19
  202.0 184.8 %all-reduce.3.cloned.1.call-done = f32[2,256,128]{2,1,0:T(8,128)} async-done(((f32[2,256,128]{2,1,0:T(8,128)}), f32[2,256,128]{2,1,0:T(8,128)}) %all-reduce.3.cloned.1.call-update) | async-done | bytes 262160
  386.8 1.3 constant_dynamic-slice_fusion
  (12 shorter events, 0.1 us)
Async XLA Ops:
  7.2 94.6 %all-gather.10.cloned.1.call-start = ((), (), s32[]{:S(2)}) async-start(), calls=%async_computation.2 | async-start | bytes 2641920 | tf_op jit(solution)/shard_map/all_gather | solution.py:244
  12.1 132.0 %all-gather.6.cloned.1.call-start = ((), (), s32[]{:S(2)}) async-start(), calls=%async_computation | async-start | bytes 3276800 | tf_op jit(solution)/shard_map/all_gather | solution.py:250
  107.0 75.5 %all-gather.8.cloned.1.call-start = ((), (), s32[]{:S(2)}) async-start(), calls=%async_computation.1 | async-start | bytes 2621440 | tf_op jit(solution)/shard_map/all_gather | solution.py:251
  107.1 75.5 %copy-start.7 = (bf16[1024,128]{1,0:T(8,128)(2,1)S(1)}, bf16[1024,128]{1,0:T(8,128)(2,1)}, u32[]{:S(2)}) copy-start(bf16[1024,128]{1,0:T(8,128)(2,1)} %t_ref.1) | copy-start | bytes 786436
  107.7 74.8 %copy-start = (bf16[1024,1536]{1,0:T(8,128)(2,1)S(1)}, bf16[1024,1536]{1,0:T(8,128)(2,1)}, u32[]{:S(2)}) copy-start(bf16[1024,1536]{1,0:T(8,128)(2,1)} %f_ref.1) | copy-start | bytes 9437188
  107.8 279.0 %all-reduce.3.cloned.1.call-start = ((), (), s32[]{:S(2)}) async-start(), calls=%async_computation.3 | async-start | bytes 524288
  144.1 1.7 copy-start.1
  166.0 0.8 copy-start.5
  182.6 1.7 copy-start.2
  184.3 1.6 copy-start.3
  185.9 1.0 copy-start.6
  196.0 1.0 copy-start.4
  197.0 0.7 copy-start.8
Sparse Core Ops, SparseCore 0:
  12.2 89.4 all-gather.9
  107.1 36.9 all-gather.5
  146.2 36.3 all-gather.7
  197.9 188.8 all-reduce.2

commit v2 on v1

--- a/solution.py
+++ b/solution.py
@@ -89,9 +89,8 @@
 
 def factor_kernel(g_ref, inv_ref, cross_ref, sq_ref):
     def gram(a, b):
-        ra, rb = slice(256 * a, 256 * a + 256), slice(256 * b, 256 * b + 256)
-        dots = sum(mm_nt(g_ref[c, ra, :FQ], g_ref[c, rb, :FQ]) for c in range(NX))
-        basis = sum(mm_nt(g_ref[c, ra, FQ:], g_ref[c, rb, FQ:]) for c in range(NX))
+        dots = sum(mm_nt(g_ref[c, a, :, :FQ], g_ref[c, b, :, :FQ]) for c in range(NX))
+        basis = sum(mm_nt(g_ref[c, a, :, FQ:], g_ref[c, b, :, FQ:]) for c in range(NX))
         return dots, basis
 
     eye = lax.broadcasted_iota(jnp.int32, (256, 256), 0) == lax.broadcasted_iota(
@@ -143,17 +142,20 @@
     return total
 
 
-def rows_kernel(place_ref, x_ref, f_ref, t_ref, g_ref, inv_ref, cross_ref, sq_ref, new_ref, res_ref, coef_ref):
-    place = place_ref[0]
+def rows_kernel(
+    x0_ref, x1_ref, x2_ref, x3_ref, f_ref, t_ref, g_ref, inv_ref, cross_ref, sq_ref,
+    new_ref, res_ref, coef_ref,
+):
+    place = lax.axis_index("cols")
     dots = jnp.zeros((TILE, 512), f32)
     basis = jnp.zeros((TILE, 512), f32)
     squares = jnp.zeros((TILE, 128), f32)
     factor_squares = jnp.zeros((TILE, 128), f32)
-    for c in range(NX):
-        x = x_ref[c]
+    for c, x_ref in enumerate((x0_ref, x1_ref, x2_ref, x3_ref)):
+        x = x_ref[...]
         fac = f_ref[:, KQ * c : KQ * c + KQ]
-        dots = dots + mm_nt(x, g_ref[c, :, :FQ])
-        basis = basis + mm_nt(fac, g_ref[c, :, FQ:])
+        dots = dots + mm_nt(x, g_ref[(place + c) % NX, :, :, :FQ].reshape(512, FQ))
+        basis = basis + mm_nt(fac, g_ref[c, :, :, FQ:].reshape(512, KQ))
         squares = squares + fold(jnp.square(x.astype(f32)))
         factor_squares = factor_squares + fold(jnp.square(fac.astype(f32)))
     sq = jnp.sum(squares, axis=1, keepdims=True)
@@ -186,21 +188,20 @@
     res0 = 1.0 - across(factor_squares + fold(jnp.square(fresh0)))
     res_ref[0:1, :] = res0
     res_ref[1:2, :] = res0 - across(fold(jnp.square(fresh1)))
-    coef_ref[:256] += mm_tn(narrow0, t_ref[...])
-    coef_ref[256:] += mm_tn(narrow1, t_ref[...])
-
-
-def solve_rows(place, x, factor, targets, g, inv, cross, sq):
+    coef_ref[0] += mm_tn(narrow0, t_ref[...])
+    coef_ref[1] += mm_tn(narrow1, t_ref[...])
+
+
+def solve_rows(xs, factor, targets, g, inv, cross, sq):
     whole = lambda shape: pl.BlockSpec(shape, lambda i: (0,) * len(shape))
     return pl.pallas_call(
         rows_kernel,
         grid=(ROWS // TILE,),
         in_specs=[
-            pl.BlockSpec(memory_space=pltpu.SMEM),
-            pl.BlockSpec((NX, TILE, FQ), lambda i: (0, i, 0)),
+            *[pl.BlockSpec((TILE, FQ), lambda i: (i, 0))] * NX,
             pl.BlockSpec((TILE, NX * KQ), lambda i: (i, 0)),
             pl.BlockSpec((TILE, 128), lambda i: (i, 0)),
-            whole((NX, 512, W)),
+            whole((NX, 2, BLOCK, W)),
             whole((2, 2, BLOCK, BLOCK)),
             whole((BLOCK, BLOCK)),
             whole((8, 512)),
@@ -208,55 +209,315 @@
         out_specs=[
             pl.BlockSpec((2, TILE, 64), lambda i: (0, i, 0)),
             pl.BlockSpec((2, TILE), lambda i: (0, i)),
-            whole((512, 128)),
+            whole((2, BLOCK, 128)),
         ],
         out_shape=(
             jax.ShapeDtypeStruct((2, ROWS, 64), f32),
             jax.ShapeDtypeStruct((2, ROWS), f32),
-            jax.ShapeDtypeStruct((512, 128), f32),
+            jax.ShapeDtypeStruct((2, BLOCK, 128), f32),
         ),
         compiler_params=pltpu.CompilerParams(vmem_limit_bytes=40 * 2**20),
         name="row_solve",
-    )(place, x, factor, targets, g, inv, cross, sq)
-
-
-def place_pivots(counts):
-    inclusive = jnp.cumsum(counts)
-    exclusive = inclusive - counts
-    pick_index = jnp.arange(BLOCK, dtype=jnp.int32)
-    owners = jnp.sum(
-        (inclusive[None, :] <= pick_index[:, None]).astype(jnp.int32), axis=1, dtype=jnp.int32
-    )
-    owner_ids = jnp.arange(counts.shape[0], dtype=jnp.int32)
-    starts = jnp.sum(
-        jnp.where(owner_ids[None, :] == owners[:, None], exclusive[None, :], 0),
-        axis=1,
-        dtype=jnp.int32,
-    )
-    return owners, pick_index - starts
+    )(*xs, factor, targets, g, inv, cross, sq)
+
+NZ = 8
+NY = 8
+CORES = 2
+MESH = pl.DeviceIdType.MESH
+
+
+def spot():
+    index = lax.axis_index("rows")
+    return index // (NY * CORES), (index // CORES) % NY, index % CORES
+
+
+def row_id(z, y, core):
+    return {"rows": (z * NY + y) * CORES + core}
+
+
+def enter(devices):
+    barrier = pltpu.get_barrier_semaphore()
+    for device in devices:
+        pl.semaphore_signal(barrier, inc=1, device_id=device, device_id_type=MESH)
+    return lambda: pl.semaphore_wait(barrier, len(devices))
+
+
+def remote(src, dst, sems, index, device):
+    return pltpu.make_async_remote_copy(
+        src_ref=src,
+        dst_ref=dst,
+        send_sem=sems.at[0, index],
+        recv_sem=sems.at[1, index],
+        device_id=device,
+        device_id_type=MESH,
+    )
+
+
+def gather_kernel(
+    slots_ref, counts_ref, points_ref, factor_ref, g_ref,
+    quarter, own, other, buf_a, buf_b, load_sem,
+    core_sem, ya_sem, zb_sem, za_sem, yb_sem, x_sem, k_sem,
+):
+    z, y, core = spot()
+    x = lax.axis_index("cols")
+    sibling = row_id(z, y, 1 - core)
+    y_peers = [row_id(z, (y + d) % NY, core) for d in range(1, NY)]
+    z_peers = [row_id((z + d) % NZ, y, core) for d in range(1, NZ)]
+    right, left = {"cols": (x + 1) % NX}, {"cols": (x + NX - 1) % NX}
+    load = pltpu.make_async_copy(
+        factor_ref.at[:, pl.ds(pl.multiple_of(x * KQ, 128), KQ)], quarter, load_sem
+    )
+    load.start()
+    wait_entered = enter([sibling] + y_peers + z_peers + [right, left])
+
+    slots = slots_ref[:, 0:1]
+    chosen = (lax.broadcasted_iota(jnp.int32, (2 * MAXP, ROWS), 1) == slots).astype(bf16)
+    own[:, :FQ] = mm_nn(chosen, points_ref[...]).astype(bf16)
+    load.wait()
+    own[:, FQ:] = mm_nn(chosen, quarter[...]).astype(bf16)
+    wait_entered()
+
+    swap = remote(own, other, core_sem, 0, sibling)
+    swap.start()
+    swap.wait()
+    mine, theirs = own[...].astype(f32), other[...].astype(f32)
+    first = core == 0
+    pair = jnp.concatenate(
+        [
+            jnp.where(first, mine[:MAXP], theirs[MAXP:]),
+            jnp.where(first, theirs[:MAXP], mine[MAXP:]),
+        ],
+        axis=0,
+    ).astype(bf16)
+    buf_a[z, y] = pair[:, FQ:]
+    buf_b[y, z] = pair[:, :FQ]
+    along_y = [
+        remote(buf_a.at[z, y], buf_a.at[z, y], ya_sem, d, y_peers[d]) for d in range(NY - 1)
+    ]
+    along_z = [
+        remote(buf_b.at[y, z], buf_b.at[y, z], zb_sem, d, z_peers[d]) for d in range(NZ - 1)
+    ]
+    for one, two in zip(along_y, along_z):
+        one.start()
+        two.start()
+
+    counts = jnp.where(first, counts_ref[0:1, :], counts_ref[1:2, :]).astype(f32)
+    counts = jnp.broadcast_to(counts, (8, 128)).astype(bf16)
+    before = lax.broadcasted_iota(jnp.int32, (128, 128), 0) < lax.broadcasted_iota(
+        jnp.int32, (128, 128), 1
+    )
+    offsets = mm_nn(counts, before.astype(bf16)).astype(bf16)
+    owner_row = lax.broadcasted_iota(jnp.int32, (128, 1024), 0)
+    column = lax.broadcasted_iota(jnp.int32, (128, 1024), 1)
+    slot = (lax.broadcasted_iota(jnp.int32, (8, 1024), 1) % MAXP).astype(f32)
+    pivot_row = lax.broadcasted_iota(jnp.int32, (BLOCK, 1024), 0)
+
+    def places(owner_of):
+        spread = (owner_row == owner_of(column // MAXP)).astype(bf16)
+        start, count = mm_nn(offsets, spread), mm_nn(counts, spread)
+        target = jnp.where(slot < count, start + slot, -1.0)
+        return (pivot_row.astype(f32) == target[0:1, :]).astype(bf16)
+
+    def swapped(position):
+        return ((position // CORES) % NZ * NY + position // (CORES * NZ)) * CORES + position % CORES
+
+    compact_a = places(lambda position: position)
+    compact_b = places(swapped)
+
+    for d in range(NY - 1):
+        source = (y + NY - 1 - d) % NY
+        remote(buf_a.at[z, source], buf_a.at[z, source], ya_sem, d, y_peers[d]).wait_recv()
+    for d in range(NZ - 1):
+        source = (z + NZ - 1 - d) % NZ
+        remote(buf_b.at[y, source], buf_b.at[y, source], zb_sem, d, z_peers[d]).wait_recv()
+
+    def ring(buf, sems, me, count, up, down):
+        ahead, back = count // 2, (count - 1) // 2
+
+        def send(step):
+            if step < ahead:
+                part = buf.at[(me + count - step) % count]
+                remote(part, part, sems, step, up).start()
+            if step < back:
+                part = buf.at[(me + step) % count]
+                remote(part, part, sems, ahead + step, down).start()
+
+        def receive(step):
+            if step < ahead:
+                part = buf.at[(me + count - 1 - step) % count]
+                remote(part, part, sems, step, up).wait_recv()
+            if step < back:
+                part = buf.at[(me + 1 + step) % count]
+                remote(part, part, sems, ahead + step, down).wait_recv()
+
+        def finish():
+            for step in range(ahead + back):
+                remote(buf.at[0], buf.at[0], sems, step, up).wait_send()
+
+        return send, receive, finish, ahead
+
+    send_a, receive_a, finish_a, steps = ring(buf_a, za_sem, z, NZ, z_peers[0], z_peers[NZ - 2])
+    send_b, receive_b, finish_b, _ = ring(buf_b, yb_sem, y, NY, y_peers[0], y_peers[NY - 2])
+    for step in range(steps):
+        send_a(step)
+        send_b(step)
+        receive_a(step)
+        receive_b(step)
+
+    g_ref[x, core, :, FQ:] = mm_nn(compact_a, buf_a[...].reshape(1024, KQ)).astype(bf16)
+    g_ref[x, core, :, :FQ] = mm_nn(compact_b, buf_b[...].reshape(1024, FQ)).astype(bf16)
+
+    half = BLOCK // 2
+    x_left, x_right, x_far = (x + NX - 1) % NX, (x + 1) % NX, (x + 2) % NX
+
+    def part(origin, at):
+        return g_ref.at[origin, core, pl.ds(at * half, half), :]
+
+    def to_right(origin, at, index):
+        return remote(part(origin, at), part(origin, at), x_sem, index, right)
+
+    def to_left(origin, at, index):
+        return remote(part(origin, at), part(origin, at), x_sem, 3 + index, left)
+
+    def to_sibling(origin):
+        return remote(g_ref.at[origin, core], g_ref.at[origin, core], k_sem, origin, sibling)
+
+    sends = [to_right(x, 0, 0), to_left(x, 1, 0), to_right(x, 1, 1), to_left(x, 0, 1), to_sibling(x)]
+    for copy in sends:
+        copy.start()
+    to_right(x_left, 0, 0).wait_recv()
+    sends.append(to_right(x_left, 0, 2))
+    sends[-1].start()
+    to_left(x_right, 1, 0).wait_recv()
+    sends.append(to_left(x_right, 1, 2))
+    sends[-1].start()
+    to_right(x_left, 1, 1).wait_recv()
+    sends.append(to_sibling(x_left))
+    sends[-1].start()
+    to_left(x_right, 0, 1).wait_recv()
+    sends.append(to_sibling(x_right))
+    sends[-1].start()
+    to_right(x_far, 0, 2).wait_recv()
+    to_left(x_far, 1, 2).wait_recv()
+    sends.append(to_sibling(x_far))
+    sends[-1].start()
+    for origin in range(NX):
+        arrived = g_ref.at[origin, 1 - core]
+        remote(arrived, arrived, k_sem, origin, sibling).wait_recv()
+    for copy in along_y + along_z + sends:
+        copy.wait_send()
+    finish_a()
+    finish_b()
+
+
+def gather_pivots(slots, counts, points, factor):
+    vmem = pl.BlockSpec(memory_space=pltpu.VMEM)
+    sems = lambda count: pltpu.SemaphoreType.DMA((2, count))
+    return pl.pallas_call(
+        gather_kernel,
+        in_specs=[vmem, vmem, vmem, pl.BlockSpec(memory_space=pl.ANY)],
+        out_specs=vmem,
+        out_shape=jax.ShapeDtypeStruct((NX, 2, BLOCK, W), bf16),
+        scratch_shapes=[
+            pltpu.VMEM((ROWS, KQ), bf16),
+            pltpu.VMEM((2 * MAXP, W), bf16),
+            pltpu.VMEM((2 * MAXP, W), bf16),
+            pltpu.VMEM((NZ, NY, 2 * MAXP, KQ), bf16),
+            pltpu.VMEM((NY, NZ, 2 * MAXP, FQ), bf16),
+            pltpu.SemaphoreType.DMA,
+            sems(1),
+            sems(NY - 1),
+            sems(NZ - 1),
+            sems(NZ - 1),
+            sems(NY - 1),
+            sems(6),
+            sems(NX),
+        ],
+        compiler_params=pltpu.CompilerParams(
+            collective_id=0, has_side_effects=True, vmem_limit_bytes=40 * 2**20
+        ),
+        name="pivot_gather",
+    )(slots, counts, points, factor)
+
+
+def sum_kernel(coef_ref, out_ref, got, total, got_z, piece, got_y, final, core_sem, z_sem, y_sem, k_sem):
+    z, y, core = spot()
+    sibling = row_id(z, y, 1 - core)
+    y_peers = [row_id(z, (y + d) % NY, core) for d in range(1, NY)]
+    z_peers = [row_id((z + d) % NZ, y, core) for d in range(1, NZ)]
+    enter([sibling] + y_peers + z_peers)()
+
+    swap = remote(coef_ref.at[1 - core], got, core_sem, 0, sibling)
+    swap.start()
+    swap.wait()
+    total[...] = (coef_ref[core] + got[...]).reshape(NZ, 32, 128)
+    over_z = [
+        remote(total.at[(z + d + 1) % NZ], got_z.at[d], z_sem, d, z_peers[d])
+        for d in range(NZ - 1)
+    ]
+    for copy in over_z:
+        copy.start()
+    for copy in over_z:
+        copy.wait()
+    mine = total[z]
+    for d in range(NZ - 1):
+        mine = mine + got_z[d]
+    piece[...] = mine.reshape(4, 8, 128)
+    over_y = [
+        remote(piece.at[(y + d + 1) % NY // 2], got_y.at[d], y_sem, d, y_peers[d])
+        for d in range(NY - 1)
+    ]
+    for copy in over_y:
+        copy.start()
+    for copy in over_y:
+        copy.wait()
+    mine = piece[y // 2]
+    for d in range(NY - 1):
+        mine = mine + got_y[d]
+    final[core] = mine
+    last = remote(final.at[core], final.at[core], k_sem, 0, sibling)
+    last.start()
+    last.wait_send()
+    remote(final.at[1 - core], final.at[1 - core], k_sem, 0, sibling).wait_recv()
+    at = (y % 2) * 4 + core * 2
+    out_ref[0] = final[0, pl.ds(at, 2), :]
+    out_ref[1] = final[1, pl.ds(at, 2), :]
+
+
+def sum_coefficients(coef):
+    vmem = pl.BlockSpec(memory_space=pltpu.VMEM)
+    sems = lambda count: pltpu.SemaphoreType.DMA((2, count))
+    return pl.pallas_call(
+        sum_kernel,
+        in_specs=[vmem],
+        out_specs=vmem,
+        out_shape=jax.ShapeDtypeStruct((2, 2, 128), f32),
+        scratch_shapes=[
+            pltpu.VMEM((BLOCK, 128), f32),
+            pltpu.VMEM((NZ, 32, 128), f32),
+            pltpu.VMEM((NZ - 1, 32, 128), f32),
+            pltpu.VMEM((4, 8, 128), f32),
+            pltpu.VMEM((NY - 1, 8, 128), f32),
+            pltpu.VMEM((2, 8, 128), f32),
+            sems(1),
+            sems(NZ - 1),
+            sems(NY - 1),
+            sems(1),
+        ],
+        compiler_params=pltpu.CompilerParams(collective_id=1, has_side_effects=True),
+        name="coefficient_sum",
+    )(coef)
 
 
 def local(points, factor, targets, pivot_slots, pivot_counts):
-    place = lax.axis_index("cols")
-    quarter = lax.dynamic_slice_in_dim(factor, place * KQ, KQ, 1)
-    rows = pivot_slots.reshape(2 * MAXP)
-    slots = jnp.concatenate([points[rows], quarter[rows]], axis=1)
-    gathered = lax.all_gather(slots, "rows", axis=0, tiled=False)
-    picks = []
-    for b in range(2):
-        owners, slot = place_pivots(pivot_counts[b])
-        picks.append(owners * 2 * MAXP + b * MAXP + slot)
-    chosen = jnp.take(gathered.reshape(-1, W), jnp.concatenate(picks), axis=0)
-    g = lax.all_gather(chosen, "cols", axis=0, tiled=False)
-    x = lax.all_gather(points, "cols", axis=0, tiled=False)
+    slots = jnp.broadcast_to(pivot_slots.reshape(2 * MAXP, 1), (2 * MAXP, 128))
+    g = gather_pivots(slots, pivot_counts, points, factor)
+    xs = [points]
+    for d in range(1, NX):
+        xs.append(lax.ppermute(points, "cols", [((i + d) % NX, i) for i in range(NX)]))
     inv, cross, sq = factor_pivots(g)
-    new, res, coef = solve_rows(
-        place.reshape(1).astype(jnp.int32), x, factor, targets, g, inv, cross, sq
-    )
-    coef = lax.psum_scatter(
-        coef.reshape(2, BLOCK, 128), "rows", scatter_dimension=1, tiled=True
-    )
-    return new, res, coef
+    new, res, coef = solve_rows(xs, factor, targets, g, inv, cross, sq)
+    return new, res, sum_coefficients(coef)
 
 
 def solution(mesh):

time: 396 us -> 120 us (0.30)
  waiting for transfers between devices: 324 us -> 0.01 us
  Pallas kernels: 29.2 us -> 100 us
  local copies, waits for them, and re-layouts: 23 us -> 7.52 us
  between operations: 14.5 us -> 0.74 us
  starting transfers between devices: 0.34 us -> 11.4 us
    unnamed x5 -> x0, waiting for transfers between devices: 185 us -> none
    all_gather x3 -> x0, waiting for transfers between devices: 139 us -> none  [the longest x1 86.7 us: local(): gathered = lax.all_gather(slots, 'rows', axis=0, tiled=False)]
    pallas_call x1 -> x3, Pallas kernels: 9.08 us -> 79.9 us  [the longest x1 51.6 us: gather_pivots(): pl.pallas_call(gather_kernel, in_specs=[vmem, vmem, vmem, pl.BlockSpec(me...]
    ppermute x0 -> x3, starting transfers between devices: none -> 11.4 us  [local(): lax.ppermute(points, 'cols', [((i + d) % NX, i) for i in range(NX)])]
    unnamed x21 -> x14, local copies, waits for them, and re-layouts: 13.5 us -> 6.69 us
    gather x3 -> x0, local copies, waits for them, and re-layouts: 6.49 us -> none  [the longest x1 4.21 us: local(): chosen = jnp.take(gathered.reshape(-1, W), jnp.concatenate(picks), axis=0)]
  transfers between devices with their start and end apart: 4 -> 3, of which waited for: 4 -> 0; matrix products, arithmetic and copies ran while one was open for 2% -> 1% of each run, Pallas kernels for 5% -> 60%
where the time goes in v2:
time: 120 us
  Pallas kernels  100 us (83%)
  starting transfers between devices  11.4 us (10%)
  local copies, waits for them, and re-layouts  7.52 us (6%)
    pallas_call x1, Pallas kernels, gather_pivots(): pl.pallas_call(gather_kernel, in_specs=[vmem, vmem, vmem, pl.BlockSpec(me...  51.6 us
    pallas_call x1, Pallas kernels, factor_pivots(): pl.pallas_call(factor_kernel, out_shape=(jax.ShapeDtypeStruct((2, 2, BLOC...  20.1 us
    pallas_call x1, Pallas kernels, sum_coefficients(): pl.pallas_call(sum_kernel, in_specs=[vmem], out_specs=vmem, out_shape=jax...  19.3 us
    ppermute x3, starting transfers between devices, local(): lax.ppermute(points, 'cols', [((i + d) % NX, i) for i in range(NX)])  11.4 us
    pallas_call x1, Pallas kernels, solve_rows(): pl.pallas_call(rows_kernel, grid=(ROWS // TILE,), in_specs=[*[pl.BlockSpe...  9.04 us
    unnamed x14, local copies, waits for them, and re-layouts  6.69 us
  transfers between devices with their start and end apart: 3, of which 0 were waited for; matrix products, arithmetic and copies ran while one was open for 1% of the time, Pallas kernels for 60%

profile of v2, /device:TPU:1, one launch (start us, length us, event | category | flops | bytes accessed | tf_op | source)
XLA Modules:
  0.0 119.6 jit_solution(9768383238133270331)
XLA Ops:
  0.6 4.0 %collective-permute-start.2 = (bf16[1024,256]{1,0:T(8,128)(2,1)}, bf16[1024,256]{1,0:T(8,128)(2,1)S(1)}, u32[]{:S(2)}, u32[]{:S(2)}) collective-permute-start(bf16[1024,256]{1,0:T(8,128)(2,1)} %x0_ref.1), channel_id=1, source_target_pairs={{3,0},{0,1},{1,2},{2,3},{7,4},{4,5},{5,6},{6,7},{11,8},{8,9},{9,10... | collective-permute-start | bytes 1572872 | tf_op jit(solution)/shard_map/ppermute | solution.py:517
  4.6 4.4 %collective-permute-start.1 = (bf16[1024,256]{1,0:T(8,128)(2,1)}, bf16[1024,256]{1,0:T(8,128)(2,1)S(1)}, u32[]{:S(2)}, u32[]{:S(2)}) collective-permute-start(bf16[1024,256]{1,0:T(8,128)(2,1)} %x0_ref.1), channel_id=1, source_target_pairs={{2,0},{3,1},{0,2},{1,3},{6,4},{7,5},{4,6},{5,7},{10,8},{11,9},{8,1... | collective-permute-start | bytes 1572872 | tf_op jit(solution)/shard_map/ppermute | solution.py:517
  9.0 3.1 %collective-permute-start = (bf16[1024,256]{1,0:T(8,128)(2,1)}, bf16[1024,256]{1,0:T(8,128)(2,1)S(1)}, u32[]{:S(2)}, u32[]{:S(2)}) collective-permute-start(bf16[1024,256]{1,0:T(8,128)(2,1)} %x0_ref.1), channel_id=1, source_target_pairs={{1,0},{2,1},{3,2},{0,3},{5,4},{6,5},{7,6},{4,7},{9,8},{10,9},{11,1... | collective-permute-start | bytes 1572872 | tf_op jit(solution)/shard_map/ppermute | solution.py:517
  12.0 0.8 broadcast_in_dim.7
  12.8 0.1 broadcast_in_dim.8.slots_ref
  12.9 0.0 copy-start
  12.9 1.9 %copy-done = bf16[1024,1536]{1,0:T(8,128)(2,1)S(1)} copy-done((bf16[1024,1536]{1,0:T(8,128)(2,1)S(1)}, bf16[1024,1536]{1,0:T(8,128)(2,1)}, u32[]{:S(2)}) %copy-start) | copy-done | bytes 3145752
  14.8 0.0 copy-start.2
  14.8 1.0 copy-done.2
  15.8 0.0 copy-start.5
  15.8 0.7 copy-done.5
  16.5 51.6 %pivot_gather.1.g_ref = bf16[4,2,256,640]{3,2,1,0:T(8,128)(2,1)S(1)} custom-call(s32[16,128]{1,0:T(8,128)S(1)} %broadcast_in_dim.8.slots_ref, s32[2,128]{1,0:T(2,128)S(1)} %copy-done.5, bf16[1024,256]{1,0:T(8,128)(2,1)S(1)} %copy-done.2, bf16[1024,1536]{1,0:T(8,128)(2,1)S(1)} %copy-done), custom_call_target="tpu_custom_call" | custom-call | tf_op jit(solution)/shard_map/pivot_gather/pallas_call | solution.py:416
  68.1 0.0 copy-start.1
  68.1 0.0 copy-start.3
  68.1 20.1 %pivot_factor.1 = (bf16[2,2,256,256]{3,2,1,0:T(8,128)(2,1)S(1)}, bf16[256,256]{1,0:T(8,128)(2,1)S(1)}, f32[8,512]{1,0:T(8,128)S(1)}) custom-call(bf16[4,2,256,640]{3,2,1,0:T(8,128)(2,1)S(1)} %pivot_gather.1.g_ref), custom_call_target="tpu_custom_call" | custom-call | flops 60000002048 | bytes 4000000 | tf_op jit(solution)/shard_map/pivot_factor/pallas_call | solution.py:123
  88.2 0.0 collective-permute-done.2.x3_ref
  88.2 0.0 collective-permute-done.1.x2_ref
  88.2 0.0 collective-permute-done.x1_ref
  88.2 0.0 copy-done.1
  88.3 0.0 copy-done.3
  88.3 9.0 %row_solve.1 = (f32[2,1024,64]{2,1,0:T(8,128)S(1)}, f32[2,1024]{1,0:T(2,128)}, f32[2,256,128]{2,1,0:T(8,128)S(1)}) custom-call(bf16[1024,256]{1,0:T(8,128)(2,1)S(1)} %copy-done.2, bf16[1024,256]{1,0:T(8,128)(2,1)S(1)} %collective-permute-done.x1_ref, bf16[1024,256]{1,0:T(8,128)(2,1)S(1)} %collective-permute-done.1.x2_ref, ...), custom_call_target="tpu_custom_call" | custom-call | tf_op jit(solution)/shard_map/row_solve/pallas_call | solution.py:197
  97.3 0.0 copy-start.4
  97.3 0.7 copy-done.4
  98.0 1.1 copy.8
  99.1 19.3 %coefficient_sum.1 = f32[2,2,128]{2,1,0:T(2,128)} custom-call(f32[2,256,128]{2,1,0:T(8,128)} %copy-done.4), custom_call_target="tpu_custom_call" | custom-call | tf_op jit(solution)/shard_map/coefficient_sum/pallas_call | solution.py:490
  118.4 1.2 %copy.10 = f32[2,2,128]{2,1,0:T(2,128)} copy(f32[2,2,128]{2,1,0:T(2,128)} %coefficient_sum.1) | data formatting | bytes 4096
Async XLA Ops:
  0.6 87.6 %collective-permute-start.2 = (bf16[1024,256]{1,0:T(8,128)(2,1)}, bf16[1024,256]{1,0:T(8,128)(2,1)S(1)}, u32[]{:S(2)}, u32[]{:S(2)}) collective-permute-start(bf16[1024,256]{1,0:T(8,128)(2,1)} %x0_ref.1), channel_id=1, source_target_pairs={{3,0},{0,1},{1,2},{2,3},{7,4},{4,5},{5,6},{6,7},{11,8},{8,9},{9,10... | collective-permute-start | bytes 1572872 | tf_op jit(solution)/shard_map/ppermute | solution.py:517
  4.6 83.6 %collective-permute-start.1 = (bf16[1024,256]{1,0:T(8,128)(2,1)}, bf16[1024,256]{1,0:T(8,128)(2,1)S(1)}, u32[]{:S(2)}, u32[]{:S(2)}) collective-permute-start(bf16[1024,256]{1,0:T(8,128)(2,1)} %x0_ref.1), channel_id=1, source_target_pairs={{2,0},{3,1},{0,2},{1,3},{6,4},{7,5},{4,6},{5,7},{10,8},{11,9},{8,1... | collective-permute-start | bytes 1572872 | tf_op jit(solution)/shard_map/ppermute | solution.py:517
  9.0 79.3 %collective-permute-start = (bf16[1024,256]{1,0:T(8,128)(2,1)}, bf16[1024,256]{1,0:T(8,128)(2,1)S(1)}, u32[]{:S(2)}, u32[]{:S(2)}) collective-permute-start(bf16[1024,256]{1,0:T(8,128)(2,1)} %x0_ref.1), channel_id=1, source_target_pairs={{1,0},{2,1},{3,2},{0,3},{5,4},{6,5},{7,6},{4,7},{9,8},{10,9},{11,1... | collective-permute-start | bytes 1572872 | tf_op jit(solution)/shard_map/ppermute | solution.py:517
  12.9 1.9 %copy-start = (bf16[1024,1536]{1,0:T(8,128)(2,1)S(1)}, bf16[1024,1536]{1,0:T(8,128)(2,1)}, u32[]{:S(2)}) copy-start(bf16[1024,1536]{1,0:T(8,128)(2,1)} %f_ref.1) | copy-start | bytes 9437188
  14.8 1.0 copy-start.2
  15.8 0.7 copy-start.5
  68.1 20.2 %copy-start.1 = (bf16[1024,1536]{1,0:T(8,128)(2,1)S(1)}, bf16[1024,1536]{1,0:T(8,128)(2,1)}, u32[]{:S(2)}) copy-start(bf16[1024,1536]{1,0:T(8,128)(2,1)} %f_ref.1) | copy-start | bytes 9437188
  68.1 20.2 %copy-start.3 = (bf16[1024,128]{1,0:T(8,128)(2,1)S(1)}, bf16[1024,128]{1,0:T(8,128)(2,1)}, u32[]{:S(2)}) copy-start(bf16[1024,128]{1,0:T(8,128)(2,1)} %t_ref.1) | copy-start | bytes 786436
  97.3 0.7 copy-start.4

commit v3 on v2

--- a/solution.py
+++ b/solution.py
@@ -106,8 +106,8 @@
     dots11, basis11 = gram(1, 1)
     col0, row0 = norms(dots00)
     col1, row1 = norms(dots11)
-    sq_ref[:, :256] = jnp.broadcast_to(row0, (8, 256))
-    sq_ref[:, 256:] = jnp.broadcast_to(row1, (8, 256))
+    sq_ref[:256] = jnp.broadcast_to(col0, (256, 128))
+    sq_ref[256:] = jnp.broadcast_to(col1, (256, 128))
     a00 = jnp.exp(-(col0 + row0 - 2.0 * dots00) / F) - basis00
     a10 = jnp.exp(-(col1 + row0 - 2.0 * dots10) / F) - basis10
     a11 = jnp.exp(-(col1 + row1 - 2.0 * dots11) / F) - basis11
@@ -125,7 +125,7 @@
         out_shape=(
             jax.ShapeDtypeStruct((2, 2, BLOCK, BLOCK), bf16),
             jax.ShapeDtypeStruct((BLOCK, BLOCK), bf16),
-            jax.ShapeDtypeStruct((8, 2 * BLOCK), f32),
+            jax.ShapeDtypeStruct((2 * BLOCK, 128), f32),
         ),
         compiler_params=pltpu.CompilerParams(vmem_limit_bytes=40 * 2**20),
         cost_estimate=pl.CostEstimate(
@@ -144,52 +144,48 @@
 
 def rows_kernel(
     x0_ref, x1_ref, x2_ref, x3_ref, f_ref, t_ref, g_ref, inv_ref, cross_ref, sq_ref,
-    new_ref, res_ref, coef_ref,
+    new_ref, res_ref, coef_ref, all_ref,
 ):
     place = lax.axis_index("cols")
-    dots = jnp.zeros((TILE, 512), f32)
-    basis = jnp.zeros((TILE, 512), f32)
+    dots = jnp.zeros((2 * BLOCK, TILE), f32)
+    basis = jnp.zeros((2 * BLOCK, TILE), f32)
     squares = jnp.zeros((TILE, 128), f32)
     factor_squares = jnp.zeros((TILE, 128), f32)
     for c, x_ref in enumerate((x0_ref, x1_ref, x2_ref, x3_ref)):
         x = x_ref[...]
         fac = f_ref[:, KQ * c : KQ * c + KQ]
-        dots = dots + mm_nt(x, g_ref[(place + c) % NX, :, :, :FQ].reshape(512, FQ))
-        basis = basis + mm_nt(fac, g_ref[c, :, :, FQ:].reshape(512, KQ))
+        dots = dots + mm_nt(g_ref[(place + c) % NX, :, :, :FQ].reshape(2 * BLOCK, FQ), x)
+        basis = basis + mm_nt(g_ref[c, :, :, FQ:].reshape(2 * BLOCK, KQ), fac)
         squares = squares + fold(jnp.square(x.astype(f32)))
         factor_squares = factor_squares + fold(jnp.square(fac.astype(f32)))
-    sq = jnp.sum(squares, axis=1, keepdims=True)
-    columns = jnp.exp(-(sq + sq_ref[0:1, :] - 2.0 * dots) / F) - basis
+
+    def across(v):
+        return jnp.sum(jnp.transpose(v), axis=0, keepdims=True)
+
+    columns = jnp.exp(-(sq_ref[:, 0:1] + across(squares) - 2.0 * dots) / F) - basis
 
     def solve(b, cols):
         high, low = split2(cols)
         return (
-            mm_nt(high, inv_ref[b, 0]) + mm_nt(high, inv_ref[b, 1]) + mm_nt(low, inv_ref[b, 0])
+            mm_nn(inv_ref[b, 0], high) + mm_nn(inv_ref[b, 1], high) + mm_nn(inv_ref[b, 0], low)
         )
-
-    def keep(b, fresh):
-        half = jnp.where(place >= 2, fresh[:, 128:], fresh[:, :128])
-        part = jnp.where(place % 2 == 1, pltpu.roll(half, 64, 1), half)
-        new_ref[b] = part[:, :64]
-
-    def across(v):
-        return jnp.sum(jnp.transpose(v), axis=0, keepdims=True)
 
     @pl.when(pl.program_id(0) == 0)
     def _():
         coef_ref[...] = jnp.zeros_like(coef_ref)
 
-    fresh0 = solve(0, columns[:, :256])
-    narrow0 = fresh0.astype(bf16)
-    fresh1 = solve(1, columns[:, 256:] - mm_nt(narrow0, cross_ref[...]))
-    narrow1 = fresh1.astype(bf16)
-    keep(0, fresh0)
-    keep(1, fresh1)
-    res0 = 1.0 - across(factor_squares + fold(jnp.square(fresh0)))
-    res_ref[0:1, :] = res0
-    res_ref[1:2, :] = res0 - across(fold(jnp.square(fresh1)))
-    coef_ref[0] += mm_tn(narrow0, t_ref[...])
-    coef_ref[1] += mm_tn(narrow1, t_ref[...])
+    res = 1.0 - across(factor_squares)
+    cols = columns[:BLOCK]
+    for b in range(2):
+        fresh = solve(b, cols)
+        narrow = fresh.astype(bf16)
+        if b == 0:
+            cols = columns[BLOCK:] - mm_nn(cross_ref[...], narrow)
+        all_ref[...] = fresh
+        new_ref[b] = all_ref[pl.ds(pl.multiple_of(place * 64, 64), 64), :]
+        res = res - jnp.sum(jnp.square(fresh), axis=0, keepdims=True)
+        res_ref[b : b + 1, :] = res
+        coef_ref[b] += mm_nn(narrow, t_ref[...])
 
 
 def solve_rows(xs, factor, targets, g, inv, cross, sq):
@@ -204,18 +200,19 @@
             whole((NX, 2, BLOCK, W)),
             whole((2, 2, BLOCK, BLOCK)),
             whole((BLOCK, BLOCK)),
-            whole((8, 512)),
+            whole((2 * BLOCK, 128)),
         ],
         out_specs=[
-            pl.BlockSpec((2, TILE, 64), lambda i: (0, i, 0)),
+            pl.BlockSpec((2, 64, TILE), lambda i: (0, 0, i)),
             pl.BlockSpec((2, TILE), lambda i: (0, i)),
             whole((2, BLOCK, 128)),
         ],
         out_shape=(
-            jax.ShapeDtypeStruct((2, ROWS, 64), f32),
+            jax.ShapeDtypeStruct((2, 64, ROWS), f32),
             jax.ShapeDtypeStruct((2, ROWS), f32),
             jax.ShapeDtypeStruct((2, BLOCK, 128), f32),
         ),
+        scratch_shapes=[pltpu.VMEM((BLOCK, TILE), f32)],
         compiler_params=pltpu.CompilerParams(vmem_limit_bytes=40 * 2**20),
         name="row_solve",
     )(*xs, factor, targets, g, inv, cross, sq)
@@ -223,6 +220,7 @@
 NZ = 8
 NY = 8
 CORES = 2
+PARTS = 4
 MESH = pl.DeviceIdType.MESH
 
 
@@ -254,9 +252,9 @@
 
 
 def gather_kernel(
-    slots_ref, counts_ref, points_ref, factor_ref, g_ref,
-    quarter, own, other, buf_a, buf_b, load_sem,
-    core_sem, ya_sem, zb_sem, za_sem, yb_sem, x_sem, k_sem,
+    slots_ref, counts_ref, points_ref, factor_ref, g_ref, x1_ref, x2_ref, x3_ref,
+    mine_points, quarter, own, other, buf_a, buf_b, load_sem,
+    core_sem, ya_sem, zb_sem, za_sem, yb_sem, x_sem, k_sem, p_sem,
 ):
     z, y, core = spot()
     x = lax.axis_index("cols")
@@ -264,21 +262,43 @@
     y_peers = [row_id(z, (y + d) % NY, core) for d in range(1, NY)]
     z_peers = [row_id((z + d) % NZ, y, core) for d in range(1, NZ)]
     right, left = {"cols": (x + 1) % NX}, {"cols": (x + NX - 1) % NX}
-    load = pltpu.make_async_copy(
-        factor_ref.at[:, pl.ds(pl.multiple_of(x * KQ, 128), KQ)], quarter, load_sem
-    )
-    load.start()
+    loads = [
+        pltpu.make_async_copy(
+            factor_ref.at[:, pl.ds(pl.multiple_of(x * KQ, 128), KQ)], quarter, load_sem.at[0]
+        ),
+        pltpu.make_async_copy(points_ref, mine_points, load_sem.at[1]),
+    ]
+    for load in loads:
+        load.start()
     wait_entered = enter([sibling] + y_peers + z_peers + [right, left])
 
-    slots = slots_ref[:, 0:1]
-    chosen = (lax.broadcasted_iota(jnp.int32, (2 * MAXP, ROWS), 1) == slots).astype(bf16)
-    own[:, :FQ] = mm_nn(chosen, points_ref[...]).astype(bf16)
-    load.wait()
+    diagonal = lax.broadcasted_iota(jnp.int32, (MAXP, MAXP), 0) == lax.broadcasted_iota(
+        jnp.int32, (MAXP, MAXP), 1
+    )
+    slots = [
+        jnp.sum(
+            jnp.where(diagonal, slots_ref[b : b + 1, :].astype(f32), 0.0), axis=1, keepdims=True
+        ).astype(jnp.int32)
+        for b in range(2)
+    ]
+    point = lax.broadcasted_iota(jnp.int32, (MAXP, ROWS), 1)
+    chosen = jnp.concatenate([(point == slot).astype(f32) for slot in slots], axis=0).astype(bf16)
+    for load in loads:
+        load.wait()
+    own[:, :FQ] = mm_nn(chosen, mine_points[...]).astype(bf16)
     own[:, FQ:] = mm_nn(chosen, quarter[...]).astype(bf16)
     wait_entered()
 
     swap = remote(own, other, core_sem, 0, sibling)
     swap.start()
+    far_half = ROWS // 2
+    low, high = pl.ds(0, far_half), pl.ds(far_half, far_half)
+    points_left = remote(points_ref, x1_ref, p_sem, 0, left)
+    points_right = remote(points_ref, x3_ref, p_sem, 1, right)
+    far_left = remote(x1_ref.at[low], x2_ref.at[low], p_sem, 2, left)
+    far_right = remote(x3_ref.at[high], x2_ref.at[high], p_sem, 3, right)
+    points_left.start()
+    points_right.start()
     swap.wait()
     mine, theirs = own[...].astype(f32), other[...].astype(f32)
     first = core == 0
@@ -332,37 +352,60 @@
         remote(buf_b.at[y, source], buf_b.at[y, source], zb_sem, d, z_peers[d]).wait_recv()
 
     def ring(buf, sems, me, count, up, down):
-        ahead, back = count // 2, (count - 1) // 2
-
-        def send(step):
-            if step < ahead:
-                part = buf.at[(me + count - step) % count]
-                remote(part, part, sems, step, up).start()
-            if step < back:
-                part = buf.at[(me + step) % count]
-                remote(part, part, sems, ahead + step, down).start()
-
-        def receive(step):
-            if step < ahead:
-                part = buf.at[(me + count - 1 - step) % count]
-                remote(part, part, sems, step, up).wait_recv()
-            if step < back:
-                part = buf.at[(me + 1 + step) % count]
-                remote(part, part, sems, ahead + step, down).wait_recv()
+        last = count // 2 - 1
+        size = buf.shape[1] // PARTS
+
+        def go_up(step, part, origin):
+            piece = buf.at[origin % count, pl.ds(part * size, size)]
+            return remote(piece, piece, sems, step * PARTS + part, up)
+
+        def go_down(step, part, origin):
+            piece = buf.at[origin % count, pl.ds(part * size, size)]
+            return remote(piece, piece, sems, (last + 1 + step) * PARTS + part, down)
+
+        goes_up = lambda step, part: step < last or part < PARTS // 2
+        goes_down = lambda step, part: step < last or part >= PARTS // 2
+
+        def send(step, part):
+            if goes_up(step, part):
+                go_up(step, part, me + count - step).start()
+            if goes_down(step, part):
+                go_down(step, part, me + step).start()
+
+        def receive(step, part):
+            if goes_up(step, part):
+                go_up(step, part, me + count - 1 - step).wait_recv()
+            if goes_down(step, part):
+                go_down(step, part, me + 1 + step).wait_recv()
 
         def finish():
-            for step in range(ahead + back):
-                remote(buf.at[0], buf.at[0], sems, step, up).wait_send()
-
-        return send, receive, finish, ahead
-
-    send_a, receive_a, finish_a, steps = ring(buf_a, za_sem, z, NZ, z_peers[0], z_peers[NZ - 2])
-    send_b, receive_b, finish_b, _ = ring(buf_b, yb_sem, y, NY, y_peers[0], y_peers[NY - 2])
-    for step in range(steps):
-        send_a(step)
-        send_b(step)
-        receive_a(step)
-        receive_b(step)
+            for step in range(last + 1):
+                for part in range(PARTS):
+                    if goes_up(step, part):
+                        go_up(step, part, me + count - step).wait_send()
+                    if goes_down(step, part):
+                        go_down(step, part, me + step).wait_send()
+
+        return send, receive, finish
+
+    rings = [
+        ring(buf_a, za_sem, z, NZ, z_peers[0], z_peers[NZ - 2]),
+        ring(buf_b, yb_sem, y, NY, y_peers[0], y_peers[NY - 2]),
+    ]
+    for part in range(PARTS):
+        for send, receive, finish in rings:
+            send(0, part)
+    for step in range(NZ // 2):
+        for part in range(PARTS):
+            for send, receive, finish in rings:
+                receive(step, part)
+                if step + 1 < NZ // 2:
+                    send(step + 1, part)
+        if step == 1:
+            points_left.wait_recv()
+            far_left.start()
+            points_right.wait_recv()
+            far_right.start()
 
     g_ref[x, core, :, FQ:] = mm_nn(compact_a, buf_a[...].reshape(1024, KQ)).astype(bf16)
     g_ref[x, core, :, :FQ] = mm_nn(compact_b, buf_b[...].reshape(1024, FQ)).astype(bf16)
@@ -406,46 +449,55 @@
         remote(arrived, arrived, k_sem, origin, sibling).wait_recv()
     for copy in along_y + along_z + sends:
         copy.wait_send()
-    finish_a()
-    finish_b()
+    for send, receive, finish in rings:
+        finish()
+    points_left.wait_send()
+    points_right.wait_send()
+    far_left.wait()
+    far_right.wait()
 
 
 def gather_pivots(slots, counts, points, factor):
     vmem = pl.BlockSpec(memory_space=pltpu.VMEM)
+    hbm = pl.BlockSpec(memory_space=pltpu.HBM)
     sems = lambda count: pltpu.SemaphoreType.DMA((2, count))
+    shape = jax.ShapeDtypeStruct((ROWS, FQ), bf16)
     return pl.pallas_call(
         gather_kernel,
-        in_specs=[vmem, vmem, vmem, pl.BlockSpec(memory_space=pl.ANY)],
-        out_specs=vmem,
-        out_shape=jax.ShapeDtypeStruct((NX, 2, BLOCK, W), bf16),
+        in_specs=[vmem, vmem, hbm, hbm],
+        out_specs=[vmem, hbm, hbm, hbm],
+        out_shape=(jax.ShapeDtypeStruct((NX, 2, BLOCK, W), bf16), shape, shape, shape),
         scratch_shapes=[
+            pltpu.VMEM((ROWS, FQ), bf16),
             pltpu.VMEM((ROWS, KQ), bf16),
             pltpu.VMEM((2 * MAXP, W), bf16),
             pltpu.VMEM((2 * MAXP, W), bf16),
             pltpu.VMEM((NZ, NY, 2 * MAXP, KQ), bf16),
             pltpu.VMEM((NY, NZ, 2 * MAXP, FQ), bf16),
-            pltpu.SemaphoreType.DMA,
+            pltpu.SemaphoreType.DMA((2,)),
             sems(1),
             sems(NY - 1),
             sems(NZ - 1),
-            sems(NZ - 1),
-            sems(NY - 1),
+            sems(NZ * PARTS),
+            sems(NY * PARTS),
             sems(6),
             sems(NX),
+            sems(4),
         ],
         compiler_params=pltpu.CompilerParams(
-            collective_id=0, has_side_effects=True, vmem_limit_bytes=40 * 2**20
+            collective_id=0, has_side_effects=True, vmem_limit_bytes=60 * 2**20
         ),
         name="pivot_gather",
     )(slots, counts, points, factor)
 
 
-def sum_kernel(coef_ref, out_ref, got, total, got_z, piece, got_y, final, core_sem, z_sem, y_sem, k_sem):
+def sum_kernel(coef_ref, out_ref, got, total, got_z, piece, got_y, final, core_sem, z_sem, y_sem):
     z, y, core = spot()
     sibling = row_id(z, y, 1 - core)
-    y_peers = [row_id(z, (y + d) % NY, core) for d in range(1, NY)]
     z_peers = [row_id((z + d) % NZ, y, core) for d in range(1, NZ)]
-    enter([sibling] + y_peers + z_peers)()
+    y_same = [row_id(z, (y + d) % NY, core) for d in range(1, NY)]
+    y_other = [row_id(z, (y + d) % NY, 1 - core) for d in range(NY)]
+    enter(z_peers + y_same + y_other)()
 
     swap = remote(coef_ref.at[1 - core], got, core_sem, 0, sibling)
     swap.start()
@@ -463,25 +515,29 @@
     for d in range(NZ - 1):
         mine = mine + got_z[d]
     piece[...] = mine.reshape(4, 8, 128)
-    over_y = [
-        remote(piece.at[(y + d + 1) % NY // 2], got_y.at[d], y_sem, d, y_peers[d])
-        for d in range(NY - 1)
-    ]
+    over_y = []
+    for d in range(NY):
+        tile = piece.at[(y + d) % NY // 2]
+        if d:
+            over_y.append(remote(tile, got_y.at[core, d], y_sem, d, y_same[d - 1]))
+        over_y.append(remote(tile, got_y.at[core, d], y_sem, NY + d, y_other[d]))
     for copy in over_y:
         copy.start()
-    for copy in over_y:
-        copy.wait()
-    mine = piece[y // 2]
-    for d in range(NY - 1):
-        mine = mine + got_y[d]
-    final[core] = mine
-    last = remote(final.at[core], final.at[core], k_sem, 0, sibling)
-    last.start()
-    last.wait_send()
-    remote(final.at[1 - core], final.at[1 - core], k_sem, 0, sibling).wait_recv()
+    got_y[core, 0] = piece[y // 2]
+    for d in range(NY):
+        if d:
+            remote(piece.at[0], got_y.at[core, d], y_sem, d, y_same[d - 1]).wait_recv()
+        remote(piece.at[0], got_y.at[1 - core, d], y_sem, NY + d, y_other[d]).wait_recv()
+    for b in range(2):
+        mine = got_y[b, 0]
+        for d in range(1, NY):
+            mine = mine + got_y[b, d]
+        final[b] = mine
     at = (y % 2) * 4 + core * 2
     out_ref[0] = final[0, pl.ds(at, 2), :]
     out_ref[1] = final[1, pl.ds(at, 2), :]
+    for copy in over_y:
+        copy.wait_send()
 
 
 def sum_coefficients(coef):
@@ -497,12 +553,11 @@
             pltpu.VMEM((NZ, 32, 128), f32),
             pltpu.VMEM((NZ - 1, 32, 128), f32),
             pltpu.VMEM((4, 8, 128), f32),
-            pltpu.VMEM((NY - 1, 8, 128), f32),
+            pltpu.VMEM((2, NY, 8, 128), f32),
             pltpu.VMEM((2, 8, 128), f32),
             sems(1),
             sems(NZ - 1),
-            sems(NY - 1),
-            sems(1),
+            sems(2 * NY),
         ],
         compiler_params=pltpu.CompilerParams(collective_id=1, has_side_effects=True),
         name="coefficient_sum",
@@ -510,14 +565,10 @@
 
 
 def local(points, factor, targets, pivot_slots, pivot_counts):
-    slots = jnp.broadcast_to(pivot_slots.reshape(2 * MAXP, 1), (2 * MAXP, 128))
-    g = gather_pivots(slots, pivot_counts, points, factor)
-    xs = [points]
-    for d in range(1, NX):
-        xs.append(lax.ppermute(points, "cols", [((i + d) % NX, i) for i in range(NX)]))
+    g, *others = gather_pivots(pivot_slots, pivot_counts, points, factor)
     inv, cross, sq = factor_pivots(g)
-    new, res, coef = solve_rows(xs, factor, targets, g, inv, cross, sq)
-    return new, res, sum_coefficients(coef)
+    new, res, coef = solve_rows([points, *others], factor, targets, g, inv, cross, sq)
+    return jnp.swapaxes(new, 1, 2), res, sum_coefficients(coef)
 
 
 def solution(mesh):

time: 120 us -> 106 us (0.88)
  starting transfers between devices: 11.4 us -> 0 us
  local copies, waits for them, and re-layouts: 7.52 us -> 3.72 us
    ppermute x3 -> x0, starting transfers between devices: 11.4 us -> none  [local(): lax.ppermute(points, 'cols', [((i + d) % NX, i) for i in range(NX)])]
    unnamed x14 -> x19, local copies, waits for them, and re-layouts: 6.69 us -> 3.72 us
    pallas_call x1, Pallas kernels: 51.6 us -> 53.4 us  [gather_pivots(): pl.pallas_call(gather_kernel, in_specs=[vmem, vmem, hbm, hbm], out_specs=...]
  transfers between devices with their start and end apart: 3 -> 0, of which waited for: 0 -> 0; matrix products, arithmetic and copies ran while one was open for 1% -> 0% of each run, Pallas kernels for 60% -> 0%
where the time goes in v3:
time: 106 us
  Pallas kernels  101 us (95%)
  local copies, waits for them, and re-layouts  3.72 us (4%)
    pallas_call x1, Pallas kernels, gather_pivots(): pl.pallas_call(gather_kernel, in_specs=[vmem, vmem, hbm, hbm], out_specs=...  53.4 us
    pallas_call x1, Pallas kernels, factor_pivots(): pl.pallas_call(factor_kernel, out_shape=(jax.ShapeDtypeStruct((2, 2, BLOC...  20.1 us
    pallas_call x1, Pallas kernels, sum_coefficients(): pl.pallas_call(sum_kernel, in_specs=[vmem], out_specs=vmem, out_shape=jax...  18.1 us
    pallas_call x1, Pallas kernels, solve_rows(): pl.pallas_call(rows_kernel, grid=(ROWS // TILE,), in_specs=[*[pl.BlockSpe...  9.61 us
    unnamed x19, local copies, waits for them, and re-layouts  3.72 us

profile of v3, /device:TPU:1, one launch (start us, length us, event | category | flops | bytes accessed | tf_op | source)
XLA Modules:
  0.0 105.7 jit_solution(17379609331590021804)
XLA Ops:
  0.6 53.4 %pivot_gather.1 = (bf16[4,2,256,640]{3,2,1,0:T(8,128)(2,1)}, bf16[1024,256]{1,0:T(8,128)(2,1)}, bf16[1024,256]{1,0:T(8,128)(2,1)}, bf16[1024,256]{1,0:T(8,128)(2,1)}) custom-call(s32[2,8]{1,0:T(2,128)} %slots_ref.1, s32[2,128]{1,0:T(2,128)} %counts_ref.1, bf16[1024,256]{1,0:T(8,128)(2,1)} %x0_ref.1, bf16[1024,1536]{1,0:T(8,128)(2,1)} %f_ref.1), custom_call_target="tpu_custom_call" | custom-call | tf_op jit(solution)/shard_map/pivot_gather/pallas_call | solution.py:465
  54.0 0.0 copy-start.1
  54.0 1.7 %copy-done.1 = bf16[4,2,256,640]{3,2,1,0:T(8,128)(2,1)S(1)} copy-done((bf16[4,2,256,640]{3,2,1,0:T(8,128)(2,1)S(1)}, bf16[4,2,256,640]{3,2,1,0:T(8,128)(2,1)}, u32[]{:S(2)}) %copy-start.1) | copy-done | bytes 2621464
  55.8 0.0 copy-start
  55.8 0.0 copy-start.2
  55.8 0.0 copy-start.3
  55.8 0.0 copy-start.4
  55.8 0.0 copy-start.5
  55.8 0.0 copy-start.6
  55.8 0.0 copy-start.7
  55.8 20.1 %pivot_factor.1 = (bf16[2,2,256,256]{3,2,1,0:T(8,128)(2,1)S(1)}, bf16[256,256]{1,0:T(8,128)(2,1)S(1)}, f32[512,128]{1,0:T(8,128)S(1)}) custom-call(bf16[4,2,256,640]{3,2,1,0:T(8,128)(2,1)S(1)} %copy-done.1), custom_call_target="tpu_custom_call" | custom-call | flops 60000002048 | bytes 4000000 | tf_op jit(solution)/shard_map/pivot_factor/pallas_call | solution.py:123
  75.9 0.0 copy-done
  76.0 0.0 copy-done.2
  76.0 0.0 copy-done.3
  76.0 0.0 copy-done.4
  76.0 0.0 copy-done.5
  76.0 0.0 copy-done.6
  76.0 0.0 copy-done.7
  76.0 9.6 %row_solve.1 = (f32[2,64,1024]{2,1,0:T(8,128)}, f32[2,1024]{1,0:T(2,128)}, f32[2,256,128]{2,1,0:T(8,128)S(1)}) custom-call(bf16[1024,256]{1,0:T(8,128)(2,1)S(1)} %copy-done.3, bf16[1024,256]{1,0:T(8,128)(2,1)S(1)} %copy-done.4, bf16[1024,256]{1,0:T(8,128)(2,1)S(1)} %copy-done.5, bf16[1024,256]{1,0:T(8,128)(2,1)S(1)} %copy-done.6, ...), custom_call_target="tpu_custom_call" | custom-call | tf_op jit(solution)/shard_map/row_solve/pallas_call | solution.py:193
  85.6 0.0 copy-start.8
  85.6 0.7 copy-done.8
  86.3 18.1 %coefficient_sum.1 = f32[2,2,128]{2,1,0:T(2,128)} custom-call(f32[2,256,128]{2,1,0:T(8,128)} %copy-done.8), custom_call_target="tpu_custom_call" | custom-call | tf_op jit(solution)/shard_map/coefficient_sum/pallas_call | solution.py:546
  104.4 1.3 %copy.9 = f32[2,2,128]{2,1,0:T(2,128)} copy(f32[2,2,128]{2,1,0:T(2,128)} %coefficient_sum.1) | data formatting | bytes 4096
Async XLA Ops:
  54.0 1.7 %copy-start.1 = (bf16[4,2,256,640]{3,2,1,0:T(8,128)(2,1)S(1)}, bf16[4,2,256,640]{3,2,1,0:T(8,128)(2,1)}, u32[]{:S(2)}) copy-start(bf16[4,2,256,640]{3,2,1,0:T(8,128)(2,1)} %get-tuple-element.16.g_ref) | copy-start | bytes 7864324
  55.8 20.2 %copy-start = (bf16[1024,1536]{1,0:T(8,128)(2,1)S(1)}, bf16[1024,1536]{1,0:T(8,128)(2,1)}, u32[]{:S(2)}) copy-start(bf16[1024,1536]{1,0:T(8,128)(2,1)} %f_ref.1) | copy-start | bytes 9437188
  55.8 20.2 %copy-start.2 = (bf16[4,2,256,640]{3,2,1,0:T(8,128)(2,1)S(1)}, bf16[4,2,256,640]{3,2,1,0:T(8,128)(2,1)}, u32[]{:S(2)}) copy-start(bf16[4,2,256,640]{3,2,1,0:T(8,128)(2,1)} %get-tuple-element.16.g_ref) | copy-start | bytes 7864324
  55.8 20.2 %copy-start.3 = (bf16[1024,256]{1,0:T(8,128)(2,1)S(1)}, bf16[1024,256]{1,0:T(8,128)(2,1)}, u32[]{:S(2)}) copy-start(bf16[1024,256]{1,0:T(8,128)(2,1)} %x0_ref.1) | copy-start | bytes 1572868
  55.8 20.2 %copy-start.4 = (bf16[1024,256]{1,0:T(8,128)(2,1)S(1)}, bf16[1024,256]{1,0:T(8,128)(2,1)}, u32[]{:S(2)}) copy-start(bf16[1024,256]{1,0:T(8,128)(2,1)} %get-tuple-element.13.x1_ref) | copy-start | bytes 1572868
  55.8 20.2 %copy-start.5 = (bf16[1024,256]{1,0:T(8,128)(2,1)S(1)}, bf16[1024,256]{1,0:T(8,128)(2,1)}, u32[]{:S(2)}) copy-start(bf16[1024,256]{1,0:T(8,128)(2,1)} %get-tuple-element.14.x2_ref) | copy-start | bytes 1572868
  55.8 20.2 %copy-start.6 = (bf16[1024,256]{1,0:T(8,128)(2,1)S(1)}, bf16[1024,256]{1,0:T(8,128)(2,1)}, u32[]{:S(2)}) copy-start(bf16[1024,256]{1,0:T(8,128)(2,1)} %get-tuple-element.15.x3_ref) | copy-start | bytes 1572868
  55.8 20.2 %copy-start.7 = (bf16[1024,128]{1,0:T(8,128)(2,1)S(1)}, bf16[1024,128]{1,0:T(8,128)(2,1)}, u32[]{:S(2)}) copy-start(bf16[1024,128]{1,0:T(8,128)(2,1)} %t_ref.1) | copy-start | bytes 786436
  85.6 0.7 copy-start.8

commit v4 on v3

v4 whole, which is shorter than its diff:
```python
import functools
import jax
import jax.numpy as jnp
from jax import lax
from jax.experimental import pallas as pl
from jax.experimental.pallas import tpu as pltpu
from jax.sharding import PartitionSpec as P

F = 1024
BLOCK = 256
MAXP = 8
NX = 4
FQ = 256
KQ = 384
W = FQ + KQ
ROWS = 1024
TILE = 256
HI = lax.Precision.HIGHEST
f32 = jnp.float32
bf16 = jnp.bfloat16


def mm_nt(a, b, precision=None):
    return lax.dot_general(
        a, b, (((1,), (1,)), ((), ())), precision=precision, preferred_element_type=f32
    )


def mm_nn(a, b, precision=None):
    return lax.dot_general(
        a, b, (((1,), (0,)), ((), ())), precision=precision, preferred_element_type=f32
    )


def mm_tn(a, b):
    return lax.dot_general(a, b, (((0,), (0,)), ((), ())), preferred_element_type=f32)


def split2(a):
    high = a.astype(bf16)
    return high, (a - high.astype(f32)).astype(bf16)


def nothing():
    pass


def chol_inv_128(a, beside=()):
    n = 16
    beside = list(beside)
    sub = lax.broadcasted_iota(jnp.int32, (8, 128), 0)
    lane = lax.broadcasted_iota(jnp.int32, (8, 128), 1)
    A = [a[8 * r : 8 * r + 8, :] for r in range(n)]
    X = [jnp.where(lane == sub + 8 * r, 1.0, 0.0).astype(f32) for r in range(n)]
    row = lambda v, j: jnp.broadcast_to(v[j : j + 1, :], (8, 128))
    out = []
    for k in range(n):
        columns = lambda v: [
            jnp.broadcast_to(v[:, 8 * k + m : 8 * k + m + 1], (8, 128)) for m in range(8)
        ]
        panel, own_a, own_x = columns(A[k]), A[k], X[k]
        pivots = jnp.ones((8, 128), f32)
        steps = []
        for j in range(8):
            row_p = [row(panel[m], j) if m >= j else None for m in range(8)]
            inverse = 1.0 / row_p[j]
            below = jnp.where(sub > j, panel[j], 0.0)
            for m in range(j + 1, 8):
                panel[m] = panel[m] - (below * row_p[m]) * inverse
            row_a, row_x = row(own_a, j), row(own_x, j)
            steps.append((row_a, row_x, row_p, inverse))
            pivots = jnp.where(sub == j, row_p[j], pivots)
            c = below * inverse
            own_a = own_a - c * row_a
            own_x = own_x - c * row_x
        out.append(own_x * lax.rsqrt(pivots))
        for r in range(k + 1, n):
            part = columns(A[r])
            for j, (row_a, row_x, row_p, inverse) in enumerate(steps):
                c = part[j] * inverse
                A[r] = A[r] - c * row_a
                X[r] = X[r] - c * row_x
                for m in range(j + 1, 8):
                    part[m] = part[m] - c * row_p[m]
        due = (len(beside) + n - 2 - k) // (n - 1 - k) if k < n - 1 else len(beside)
        for work in beside[:due]:
            work()
        beside = beside[due:]
    return jnp.concatenate(out, axis=0)


def chol_inv_256(a, beside=((), ())):
    inv11 = chol_inv_128(a[:128, :128], beside[0])
    low21 = mm_nt(a[128:, :128], inv11, HI)
    inv22 = chol_inv_128(a[128:, 128:] - mm_nt(low21, low21, HI), beside[1])
    inv21 = -mm_nn(inv22, mm_nn(low21, inv11, HI), HI)
    zero = jnp.zeros((128, 128), f32)
    return jnp.concatenate(
        [jnp.concatenate([inv11, zero], axis=1), jnp.concatenate([inv21, inv22], axis=1)], axis=0
    )


def fold(v):
    total = v[:, :128]
    for i in range(1, v.shape[1] // 128):
        total = total + v[:, 128 * i : 128 * i + 128]
    return total


def across(v):
    return jnp.sum(jnp.transpose(v), axis=0, keepdims=True)


def solve_kernel(
    g_hbm, x_hbm, f_hbm, t_hbm, new_ref, res_ref, coef_ref,
    g_ref, x_ref, f_ref, t_ref, columns, solved, narrow, squares, block10, block11, sems,
):
    place = lax.axis_index("cols")
    loads = [
        pltpu.make_async_copy(g_hbm.at[0], g_ref.at[0], sems.at[0]),
        pltpu.make_async_copy(g_hbm.at[1], g_ref.at[1], sems.at[1]),
        pltpu.make_async_copy(x_hbm, x_ref, sems.at[2]),
        pltpu.make_async_copy(f_hbm, f_ref, sems.at[3]),
        pltpu.make_async_copy(t_hbm, t_ref, sems.at[4]),
    ]
    for load in loads:
        load.start()
    eye = lax.broadcasted_iota(jnp.int32, (BLOCK, BLOCK), 0) == lax.broadcasted_iota(
        jnp.int32, (BLOCK, BLOCK), 1
    )

    def gram(a, b):
        dots = mm_nt(g_ref[a, :, :F], g_ref[b, :, :F])
        return dots, mm_nt(g_ref[a, :, F:], g_ref[b, :, F:])

    def kernel_matrix(col, row, dots, basis):
        return jnp.exp(-(col + row - 2.0 * dots) / F) - basis

    loads[0].wait()
    dots00, basis00 = gram(0, 0)
    diag = jnp.where(eye, dots00, 0.0)
    col0, row0 = jnp.sum(diag, axis=1, keepdims=True), jnp.sum(diag, axis=0, keepdims=True)
    a00 = kernel_matrix(col0, row0, dots00, basis00)

    cols = [col0, None]

    def tile(t):
        return pl.ds(t * TILE, TILE)

    def norms(t):
        def work():
            squares[0, :, tile(t)] = across(fold(jnp.square(x_ref[tile(t), :].astype(f32))))
            res_ref[0:1, tile(t)] = 1.0 - across(fold(jnp.square(f_ref[tile(t), :].astype(f32))))
        return work

    def fill(b, t):
        def work():
            dots = mm_nt(g_ref[b, :, :F], x_ref[tile(t), :])
            basis = mm_nt(g_ref[b, :, F:], f_ref[tile(t), :])
            columns[b, :, tile(t)] = kernel_matrix(cols[b], squares[0, :, tile(t)], dots, basis)
        return work

    def solve(b, inverse, t):
        high, low = split2(columns[b, :, tile(t)])
        fresh = mm_nn(inverse[0], high) + mm_nn(inverse[1], high) + mm_nn(inverse[0], low)
        solved[:, tile(t)] = fresh
        narrow[:, tile(t)] = fresh.astype(bf16)
        before = res_ref[0:1, tile(t)]
        res_ref[b : b + 1, tile(t)] = before - jnp.sum(jnp.square(fresh), axis=0, keepdims=True)

    tiles = range(ROWS // TILE)

    def later():
        for load in loads[1:]:
            load.wait()
        dots, basis = gram(1, 1)
        diag = jnp.where(eye, dots, 0.0)
        cols[1] = jnp.sum(diag, axis=1, keepdims=True)
        row1 = jnp.sum(diag, axis=0, keepdims=True)
        block11[...] = kernel_matrix(cols[1], row1, dots, basis)
        dots, basis = gram(1, 0)
        block10[...] = kernel_matrix(cols[1], row0, dots, basis)

    inv0 = chol_inv_256(
        a00,
        (
            [nothing] * 5 + [later] + [norms(t) for t in tiles],
            [fill(b, t) for b in range(2) for t in tiles],
        ),
    )
    split0 = split2(inv0)
    narrow10 = mm_nt(block10[...], inv0, HI).astype(bf16)
    a11 = block11[...] - mm_nt(narrow10, narrow10)

    def apply0(t):
        def work():
            solve(0, split0, t)
            columns[1, :, tile(t)] = columns[1, :, tile(t)] - mm_nn(narrow10, narrow[:, tile(t)])
        return work

    def emit(b):
        def work():
            new_ref[b] = solved[pl.ds(pl.multiple_of(place * 64, 64), 64), :]
        return work

    def coefficients(b):
        def work():
            coef_ref[b] = mm_nn(narrow[...], t_ref[...])
        return work

    inv1 = chol_inv_256(a11, ([apply0(t) for t in tiles], [emit(0), coefficients(0)]))
    split1 = split2(inv1)
    for t in tiles:
        solve(1, split1, t)
    coefficients(1)()
    emit(1)()


def solve_rows(g, x, factor, targets):
    any_ = pl.BlockSpec(memory_space=pl.ANY)
    vmem = pl.BlockSpec(memory_space=pltpu.VMEM)
    return pl.pallas_call(
        solve_kernel,
        in_specs=[any_] * 4,
        out_specs=[vmem] * 3,
        out_shape=(
            jax.ShapeDtypeStruct((2, 64, ROWS), f32),
            jax.ShapeDtypeStruct((2, ROWS), f32),
            jax.ShapeDtypeStruct((2, BLOCK, 128), f32),
        ),
        scratch_shapes=[
            pltpu.VMEM((2, BLOCK, NX * W), bf16),
            pltpu.VMEM((ROWS, F), bf16),
            pltpu.VMEM((ROWS, NX * KQ), bf16),
            pltpu.VMEM((ROWS, 128), bf16),
            pltpu.VMEM((2, BLOCK, ROWS), f32),
            pltpu.VMEM((BLOCK, ROWS), f32),
            pltpu.VMEM((BLOCK, ROWS), bf16),
            pltpu.VMEM((1, 1, ROWS), f32),
            pltpu.VMEM((BLOCK, BLOCK), f32),
            pltpu.VMEM((BLOCK, BLOCK), f32),
            pltpu.SemaphoreType.DMA((5,)),
        ],
        compiler_params=pltpu.CompilerParams(vmem_limit_bytes=60 * 2**20),
        name="pivot_solve",
    )(g, x, factor, targets)


NZ = 8
NY = 8
CORES = 2
PARTS = 2
MESH = pl.DeviceIdType.MESH


def spot():
    index = lax.axis_index("rows")
    return index // (NY * CORES), (index // CORES) % NY, index % CORES


def row_id(z, y, core):
    return {"rows": (z * NY + y) * CORES + core}


def enter(devices):
    barrier = pltpu.get_barrier_semaphore()
    for device in devices:
        pl.semaphore_signal(barrier, inc=1, device_id=device, device_id_type=MESH)
    return lambda: pl.semaphore_wait(barrier, len(devices))


def remote(src, dst, sems, index, device):
    return pltpu.make_async_remote_copy(
        src_ref=src,
        dst_ref=dst,
        send_sem=sems.at[0, index],
        recv_sem=sems.at[1, index],
        device_id=device,
        device_id_type=MESH,
    )


STREAMS = (
    (0, 128, False, lambda o: FQ * o),
    (FQ, 128, True, lambda o: F + KQ * o),
    (128, 128, False, lambda o: FQ * o + 128),
    (FQ + 128, 256, True, lambda o: F + KQ * o + 128),
)


def gather_kernel(slots_ref, counts_ref, points_ref, factor_ref, g_ref, x_ref, *scratch):
    mine_points, quarter, own, other, load_sem, core_sem, p_sem = scratch[:7]
    bufs, line_sems, ring_sems, x_sems, k_sems = [scratch[7 + 4 * i : 11 + 4 * i] for i in range(5)]
    z, y, core = spot()
    x = lax.axis_index("cols")
    sibling = row_id(z, y, 1 - core)
    y_peers = [row_id(z, (y + d) % NY, core) for d in range(1, NY)]
    z_peers = [row_id((z + d) % NZ, y, core) for d in range(1, NZ)]
    right, left = {"cols": (x + 1) % NX}, {"cols": (x + NX - 1) % NX}
    x_left, x_right, x_far = (x + NX - 1) % NX, (x + 1) % NX, (x + 2) % NX

    def lanes(start, width):
        return pl.ds(pl.multiple_of(start, 128), width)

    loads = [
        pltpu.make_async_copy(factor_ref.at[:, lanes(x * KQ, KQ)], quarter, load_sem.at[0]),
        pltpu.make_async_copy(points_ref, mine_points, load_sem.at[1]),
    ]
    keep = pltpu.make_async_copy(points_ref, x_ref.at[:, lanes(x * FQ, FQ)], load_sem.at[2])
    for load in loads:
        load.start()
    wait_entered = enter([sibling] + y_peers + z_peers + [right, left])

    diagonal = lax.broadcasted_iota(jnp.int32, (MAXP, MAXP), 0) == lax.broadcasted_iota(
        jnp.int32, (MAXP, MAXP), 1
    )
    slots = [
        jnp.sum(
            jnp.where(diagonal, slots_ref[b : b + 1, :].astype(f32), 0.0), axis=1, keepdims=True
        ).astype(jnp.int32)
        for b in range(2)
    ]
    point = lax.broadcasted_iota(jnp.int32, (MAXP, ROWS), 1)
    chosen = jnp.concatenate([(point == slot).astype(f32) for slot in slots], axis=0).astype(bf16)
    for load in loads:
        load.wait()
    own[:, :FQ] = mm_nn(chosen, mine_points[...]).astype(bf16)
    own[:, FQ:] = mm_nn(chosen, quarter[...]).astype(bf16)
    wait_entered()

    swap = remote(own, other, core_sem, 0, sibling)
    swap.start()
    half_rows = ROWS // 2

    def share(index, origin, start, count, device):
        part = x_ref.at[pl.ds(start, count), lanes(origin * FQ, FQ)]
        source = points_ref if index < 2 else part
        return remote(source, part, p_sem, index, device)

    share(0, x, 0, ROWS, left).start()
    share(1, x, 0, ROWS, right).start()
    keep.start()
    swap.wait()
    mine, theirs = own[...].astype(f32), other[...].astype(f32)
    first = core == 0
    pair = jnp.concatenate(
        [
            jnp.where(first, mine[:MAXP], theirs[MAXP:]),
            jnp.where(first, theirs[:MAXP], mine[MAXP:]),
        ],
        axis=0,
    ).astype(bf16)

    lines, rings = [], []
    for i, (start, width, y_first, _) in enumerate(STREAMS):
        here, there, peers = (z, y, y_peers) if y_first else (y, z, z_peers)
        bufs[i][here, there] = pair[:, start : start + width]
        part = bufs[i].at[here, there]
        lines.append([remote(part, part, line_sems[i], d, peers[d]) for d in range(NY - 1)])
    for d in (3, 2, 4, 1, 5, 0, 6):
        for line in lines:
            line[d].start()

    counts = jnp.where(first, counts_ref[0:1, :], counts_ref[1:2, :]).astype(f32)
    counts = jnp.broadcast_to(counts, (8, 128)).astype(bf16)
    before = lax.broadcasted_iota(jnp.int32, (128, 128), 0) < lax.broadcasted_iota(
        jnp.int32, (128, 128), 1
    )
    offsets = mm_nn(counts, before.astype(bf16)).astype(bf16)
    owner_row = lax.broadcasted_iota(jnp.int32, (128, 1024), 0)
    column = lax.broadcasted_iota(jnp.int32, (128, 1024), 1)
    slot = (lax.broadcasted_iota(jnp.int32, (8, 1024), 1) % MAXP).astype(f32)
    pivot_row = lax.broadcasted_iota(jnp.int32, (BLOCK, 1024), 0)

    def places(owner_of):
        spread = (owner_row == owner_of(column // MAXP)).astype(bf16)
        start, count = mm_nn(offsets, spread), mm_nn(counts, spread)
        target = jnp.where(slot < count, start + slot, -1.0)
        return (pivot_row.astype(f32) == target[0:1, :]).astype(bf16)

    def swapped(position):
        return ((position // CORES) % NZ * NY + position // (CORES * NZ)) * CORES + position % CORES

    compact = (places(swapped), places(lambda position: position))

    for i, (start, width, y_first, _) in enumerate(STREAMS):
        here, there, peers = (z, y, y_peers) if y_first else (y, z, z_peers)
        for d in range(NY - 1):
            part = bufs[i].at[here, (there + NY - 1 - d) % NY]
            remote(part, part, line_sems[i], d, peers[d]).wait_recv()

    def ring(buf, sems, me, count, up, down):
        last = count // 2 - 1
        size = buf.shape[1] // PARTS

        def go_up(step, part, origin):
            piece = buf.at[origin % count, pl.ds(part * size, size)]
            return remote(piece, piece, sems, step * PARTS + part, up)

        def go_down(step, part, origin):
            piece = buf.at[origin % count, pl.ds(part * size, size)]
            return remote(piece, piece, sems, (last + 1 + step) * PARTS + part, down)

        goes_up = lambda step, part: step < last or part < PARTS // 2
        goes_down = lambda step, part: step < last or part >= PARTS // 2

        def send(step, part):
            if goes_up(step, part):
                go_up(step, part, me + count - step).start()
            if goes_down(step, part):
                go_down(step, part, me + step).start()

        def receive(step, part):
            if goes_up(step, part):
                go_up(step, part, me + count - 1 - step).wait_recv()
            if goes_down(step, part):
                go_down(step, part, me + 1 + step).wait_recv()

        def finish():
            for step in range(last + 1):
                for part in range(PARTS):
                    if goes_up(step, part):
                        go_up(step, part, me + count - step).wait_send()
                    if goes_down(step, part):
                        go_down(step, part, me + step).wait_send()

        return send, receive, finish

    for i, (start, width, y_first, _) in enumerate(STREAMS):
        me, peers = (z, z_peers) if y_first else (y, y_peers)
        rings.append(ring(bufs[i], ring_sems[i], me, NZ, peers[0], peers[NZ - 2]))
    pairs = ((0, 1), (2, 3))

    def go(wave, step):
        for part in range(PARTS):
            for i in pairs[wave]:
                if step:
                    rings[i][1](step - 1, part)
                if step < NZ // 2:
                    rings[i][0](step, part)

    half = BLOCK // 2
    sends = []

    def part(i, origin, at, count=half):
        place = STREAMS[i][3](origin)
        return g_ref.at[core, pl.ds(at * half, count), lanes(place, STREAMS[i][1])]

    def to_right(i, origin, at, index):
        return remote(part(i, origin, at), part(i, origin, at), x_sems[i], index, right)

    def to_left(i, origin, at, index):
        return remote(part(i, origin, at), part(i, origin, at), x_sems[i], 3 + index, left)

    def to_sibling(i, origin, index):
        block = part(i, origin, 0, BLOCK)
        return remote(block, block, k_sems[i], index, sibling)

    def begin(copy):
        sends.append(copy)
        copy.start()

    def join(wave):
        for i in pairs[wave]:
            width, y_first = STREAMS[i][1:3]
            rows = bufs[i][...].reshape(1024, width)
            placed = mm_nn(compact[int(y_first)], rows).astype(bf16)
            g_ref[core, :, lanes(STREAMS[i][3](x), width)] = placed
        for i in pairs[wave]:
            begin(to_right(i, x, 0, 0))
            begin(to_left(i, x, 1, 0))
        for i in pairs[wave]:
            begin(to_right(i, x, 1, 1))
            begin(to_left(i, x, 0, 1))
            begin(to_sibling(i, x, 0))

    def forward(wave):
        for i in pairs[wave]:
            to_right(i, x_left, 0, 0).wait_recv()
            begin(to_right(i, x_left, 0, 2))
            to_left(i, x_right, 1, 0).wait_recv()
            begin(to_left(i, x_right, 1, 2))

    def collect(wave):
        for i in pairs[wave]:
            to_right(i, x_left, 1, 1).wait_recv()
            begin(to_sibling(i, x_left, 1))
            to_left(i, x_right, 0, 1).wait_recv()
            begin(to_sibling(i, x_right, 2))

    def close(wave):
        for i in pairs[wave]:
            to_right(i, x_far, 0, 2).wait_recv()
            to_left(i, x_far, 1, 2).wait_recv()
            begin(to_sibling(i, x_far, 3))

    go(0, 0)
    go(1, 0)
    go(0, 1)
    go(0, 2)
    go(1, 1)
    share(0, x_right, 0, ROWS, left).wait_recv()
    share(2, x_right, 0, half_rows, left).start()
    share(1, x_left, 0, ROWS, right).wait_recv()
    share(3, x_left, half_rows, half_rows, right).start()
    go(0, 3)
    go(1, 2)
    go(0, 4)
    join(0)
    go(1, 3)
    forward(0)
    go(1, 4)
    join(1)
    collect(0)
    close(0)
    forward(1)
    collect(1)
    close(1)
    for i in range(len(STREAMS)):
        for index, origin in enumerate((x, x_left, x_right, x_far)):
            block = g_ref.at[1 - core, :, lanes(STREAMS[i][3](origin), STREAMS[i][1])]
            remote(block, block, k_sems[i], index, sibling).wait_recv()
    share(2, x_far, 0, half_rows, left).wait_recv()
    share(3, x_far, half_rows, half_rows, right).wait_recv()
    share(0, x, 0, ROWS, left).wait_send()
    share(1, x, 0, ROWS, right).wait_send()
    share(2, x_right, 0, half_rows, left).wait_send()
    share(3, x_left, half_rows, half_rows, right).wait_send()
    keep.wait()
    for line in lines:
        for copy in line:
            copy.wait_send()
    for copy in sends:
        copy.wait_send()
    for send, receive, finish in rings:
        finish()


def gather_pivots(slots, counts, points, factor):
    vmem = pl.BlockSpec(memory_space=pltpu.VMEM)
    hbm = pl.BlockSpec(memory_space=pltpu.HBM)
    sems = lambda count: pltpu.SemaphoreType.DMA((2, count))
    each = len(STREAMS)
    return pl.pallas_call(
        gather_kernel,
        in_specs=[vmem, vmem, hbm, hbm],
        out_specs=[vmem, hbm],
        out_shape=(
            jax.ShapeDtypeStruct((2, BLOCK, NX * W), bf16),
            jax.ShapeDtypeStruct((ROWS, F), bf16),
        ),
        scratch_shapes=[
            pltpu.VMEM((ROWS, FQ), bf16),
            pltpu.VMEM((ROWS, KQ), bf16),
            pltpu.VMEM((2 * MAXP, W), bf16),
            pltpu.VMEM((2 * MAXP, W), bf16),
            pltpu.SemaphoreType.DMA((3,)),
            sems(1),
            sems(4),
            *[pltpu.VMEM((NZ, NY, 2 * MAXP, stream[1]), bf16) for stream in STREAMS],
            *[sems(NY - 1)] * each,
            *[sems(NZ * PARTS)] * each,
            *[sems(6)] * each,
            *[sems(NX)] * each,
        ],
        compiler_params=pltpu.CompilerParams(
            collective_id=0, has_side_effects=True, vmem_limit_bytes=60 * 2**20
        ),
        name="pivot_gather",
    )(slots, counts, points, factor)


def sum_kernel(coef_ref, out_ref, got, total, got_z, piece, got_y, final, core_sem, z_sem, y_sem):
    z, y, core = spot()
    sibling = row_id(z, y, 1 - core)
    z_peers = [row_id((z + d) % NZ, y, core) for d in range(1, NZ)]
    y_same = [row_id(z, (y + d) % NY, core) for d in range(1, NY)]
    y_other = [row_id(z, (y + d) % NY, 1 - core) for d in range(NY)]
    enter(z_peers + y_same + y_other)()

    swap = remote(coef_ref.at[1 - core], got, core_sem, 0, sibling)
    swap.start()
    swap.wait()
    total[...] = (coef_ref[core] + got[...]).reshape(NZ, 32, 128)
    over_z = [
        remote(total.at[(z + d + 1) % NZ], got_z.at[d], z_sem, d, z_peers[d])
        for d in range(NZ - 1)
    ]
    for copy in over_z:
        copy.start()
    for copy in over_z:
        copy.wait()
    mine = total[z]
    for d in range(NZ - 1):
        mine = mine + got_z[d]
    piece[...] = mine.reshape(4, 8, 128)
    over_y = []
    for d in range(NY):
        tile = piece.at[(y + d) % NY // 2]
        if d:
            over_y.append(remote(tile, got_y.at[core, d], y_sem, d, y_same[d - 1]))
        over_y.append(remote(tile, got_y.at[core, d], y_sem, NY + d, y_other[d]))
    for copy in over_y:
        copy.start()
    got_y[core, 0] = piece[y // 2]
    for d in range(NY):
        if d:
            remote(piece.at[0], got_y.at[core, d], y_sem, d, y_same[d - 1]).wait_recv()
        remote(piece.at[0], got_y.at[1 - core, d], y_sem, NY + d, y_other[d]).wait_recv()
    for b in range(2):
        mine = got_y[b, 0]
        for d in range(1, NY):
            mine = mine + got_y[b, d]
        final[b] = mine
    at = (y % 2) * 4 + core * 2
    out_ref[0] = final[0, pl.ds(at, 2), :]
    out_ref[1] = final[1, pl.ds(at, 2), :]
    for copy in over_y:
        copy.wait_send()


def sum_coefficients(coef):
    vmem = pl.BlockSpec(memory_space=pltpu.VMEM)
    sems = lambda count: pltpu.SemaphoreType.DMA((2, count))
    return pl.pallas_call(
        sum_kernel,
        in_specs=[vmem],
        out_specs=vmem,
        out_shape=jax.ShapeDtypeStruct((2, 2, 128), f32),
        scratch_shapes=[
            pltpu.VMEM((BLOCK, 128), f32),
            pltpu.VMEM((NZ, 32, 128), f32),
            pltpu.VMEM((NZ - 1, 32, 128), f32),
            pltpu.VMEM((4, 8, 128), f32),
            pltpu.VMEM((2, NY, 8, 128), f32),
            pltpu.VMEM((2, 8, 128), f32),
            sems(1),
            sems(NZ - 1),
            sems(2 * NY),
        ],
        compiler_params=pltpu.CompilerParams(collective_id=1, has_side_effects=True),
        name="coefficient_sum",
    )(coef)


def local(points, factor, targets, pivot_slots, pivot_counts):
    g, x = gather_pivots(pivot_slots, pivot_counts, points, factor)
    new, res, coef = solve_rows(g, x, factor, targets)
    return jnp.swapaxes(new, 1, 2), res, sum_coefficients(coef)


def solution(mesh):
    in_specs = (P("rows", "cols"), P("rows", None), P("rows", "cols"), P(None, "rows"), P())
    out_specs = (P(None, "rows", "cols"), P(None, "rows"), P(None, "rows", "cols"))
    return jax.shard_map(local, mesh=mesh, in_specs=in_specs, out_specs=out_specs, check_vma=False)
```

time: 106 us -> 96.2 us (0.908)
  Pallas kernels: 101 us -> 94.1 us
  local copies, waits for them, and re-layouts: 3.72 us -> 1.23 us
    pallas_call x2 -> x1, Pallas kernels: 29.7 us -> 22.4 us  [solve_rows(): pl.pallas_call(solve_kernel, in_specs=[any_] * 4, out_specs=[vmem] * 3, o...]
    unnamed x19 -> x1, local copies, waits for them, and re-layouts: 3.72 us -> 1.23 us
    pallas_call x1, Pallas kernels: 53.4 us -> 54.9 us  [gather_pivots(): pl.pallas_call(gather_kernel, in_specs=[vmem, vmem, hbm, hbm], out_specs=...]
    pallas_call x1, Pallas kernels: 18.1 us -> 16.7 us  [sum_coefficients(): pl.pallas_call(sum_kernel, in_specs=[vmem], out_specs=vmem, out_shape=jax...]
where the time goes in v4:
time: 96.2 us; the launch traced here: 95.9 us
  Pallas kernels  94.1 us (98%)
  local copies, waits for them, and re-layouts  1.23 us (1%)
    pallas_call x1, Pallas kernels, gather_pivots(): pl.pallas_call(gather_kernel, in_specs=[vmem, vmem, hbm, hbm], out_specs=...  54.9 us
    pallas_call x1, Pallas kernels, solve_rows(): pl.pallas_call(solve_kernel, in_specs=[any_] * 4, out_specs=[vmem] * 3, o...  22.4 us
    pallas_call x1, Pallas kernels, sum_coefficients(): pl.pallas_call(sum_kernel, in_specs=[vmem], out_specs=vmem, out_shape=jax...  16.7 us

profile of v4, /device:TPU:1, one launch (start us, length us, event | category | flops | bytes accessed | tf_op | source)
XLA Modules:
  0.0 95.9 jit_solution(9820216877405080099)
XLA Ops:
  0.6 54.9 %pivot_gather.1 = (bf16[2,256,2560]{2,1,0:T(8,128)(2,1)}, bf16[1024,1024]{1,0:T(8,128)(2,1)}) custom-call(s32[2,8]{1,0:T(2,128)} %slots_ref.1, s32[2,128]{1,0:T(2,128)} %counts_ref.1, bf16[1024,256]{1,0:T(8,128)(2,1)} %points_ref.1, bf16[1024,1536]{1,0:T(8,128)(2,1)} %f_hbm.1), custom_call_target="tpu_custom_call" | custom-call | tf_op jit(solution)/shard_map/pivot_gather/pallas_call | solution.py:544
  55.6 22.4 %pivot_solve.1 = (f32[2,64,1024]{2,1,0:T(8,128)}, f32[2,1024]{1,0:T(2,128)}, f32[2,256,128]{2,1,0:T(8,128)}) custom-call(bf16[2,256,2560]{2,1,0:T(8,128)(2,1)} %get-tuple-element.8.g_hbm, bf16[1024,1024]{1,0:T(8,128)(2,1)} %get-tuple-element.9.x_hbm, bf16[1024,1536]{1,0:T(8,128)(2,1)} %f_hbm.1, bf16[1024,128]{1,0:T(8,128)(2,1)} %t_hbm.1), custom_call_target="tpu_custom_call" | custom-call | tf_op jit(solution)/shard_map/pivot_solve/pallas_call | solution.py:222
  78.0 16.7 %coefficient_sum.1 = f32[2,2,128]{2,1,0:T(2,128)} custom-call(f32[2,256,128]{2,1,0:T(8,128)} %get-tuple-element.12.coef_ref), custom_call_target="tpu_custom_call" | custom-call | tf_op jit(solution)/shard_map/coefficient_sum/pallas_call | solution.py:625
  94.7 1.2 %copy.9 = f32[2,2,128]{2,1,0:T(2,128)} copy(f32[2,2,128]{2,1,0:T(2,128)} %coefficient_sum.1) | data formatting | bytes 4096

commit v5 on v4

--- a/solution.py
+++ b/solution.py
@@ -100,6 +100,10 @@
     )
 
 
+def lanes(start, width):
+    return pl.ds(pl.multiple_of(start, 128), width)
+
+
 def fold(v):
     total = v[:, :128]
     for i in range(1, v.shape[1] // 128):
@@ -112,17 +116,20 @@
 
 
 def solve_kernel(
-    g_hbm, x_hbm, f_hbm, t_hbm, new_ref, res_ref, coef_ref,
+    g_hbm, p_hbm, x_hbm, f_hbm, t_hbm, new_ref, res_ref, coef_ref,
     g_ref, x_ref, f_ref, t_ref, columns, solved, narrow, squares, block10, block11, sems,
 ):
     place = lax.axis_index("cols")
     loads = [
         pltpu.make_async_copy(g_hbm.at[0], g_ref.at[0], sems.at[0]),
         pltpu.make_async_copy(g_hbm.at[1], g_ref.at[1], sems.at[1]),
-        pltpu.make_async_copy(x_hbm, x_ref, sems.at[2]),
-        pltpu.make_async_copy(f_hbm, f_ref, sems.at[3]),
-        pltpu.make_async_copy(t_hbm, t_ref, sems.at[4]),
+        pltpu.make_async_copy(f_hbm, f_ref, sems.at[2]),
+        pltpu.make_async_copy(t_hbm, t_ref, sems.at[3]),
+        pltpu.make_async_copy(p_hbm, x_ref.at[:, lanes(place * FQ, FQ)], sems.at[4]),
     ]
+    for d in range(1, NX):
+        part = lanes((place + d) % NX * FQ, FQ)
+        loads.append(pltpu.make_async_copy(x_hbm.at[:, part], x_ref.at[:, part], sems.at[4 + d]))
     for load in loads:
         load.start()
     eye = lax.broadcasted_iota(jnp.int32, (BLOCK, BLOCK), 0) == lax.broadcasted_iota(
@@ -216,12 +223,12 @@
     emit(1)()
 
 
-def solve_rows(g, x, factor, targets):
+def solve_rows(g, points, x, factor, targets):
     any_ = pl.BlockSpec(memory_space=pl.ANY)
     vmem = pl.BlockSpec(memory_space=pltpu.VMEM)
     return pl.pallas_call(
         solve_kernel,
-        in_specs=[any_] * 4,
+        in_specs=[any_] * 5,
         out_specs=[vmem] * 3,
         out_shape=(
             jax.ShapeDtypeStruct((2, 64, ROWS), f32),
@@ -239,17 +246,18 @@
             pltpu.VMEM((1, 1, ROWS), f32),
             pltpu.VMEM((BLOCK, BLOCK), f32),
             pltpu.VMEM((BLOCK, BLOCK), f32),
-            pltpu.SemaphoreType.DMA((5,)),
+            pltpu.SemaphoreType.DMA((8,)),
         ],
         compiler_params=pltpu.CompilerParams(vmem_limit_bytes=60 * 2**20),
         name="pivot_solve",
-    )(g, x, factor, targets)
+    )(g, points, x, factor, targets)
 
 
 NZ = 8
 NY = 8
 CORES = 2
-PARTS = 2
+PARTS = 4
+RECEIVED = (NZ - 1) * PARTS
 MESH = pl.DeviceIdType.MESH
 
 
@@ -273,24 +281,24 @@
     return pltpu.make_async_remote_copy(
         src_ref=src,
         dst_ref=dst,
-        send_sem=sems.at[0, index],
-        recv_sem=sems.at[1, index],
+        send_sem=sems.at[0],
+        recv_sem=sems.at[1 + index],
         device_id=device,
         device_id_type=MESH,
     )
 
 
 STREAMS = (
-    (0, 128, False, lambda o: FQ * o),
-    (FQ, 128, True, lambda o: F + KQ * o),
-    (128, 128, False, lambda o: FQ * o + 128),
-    (FQ + 128, 256, True, lambda o: F + KQ * o + 128),
+    (0, FQ, False, lambda o: FQ * o),
+    (FQ, KQ, True, lambda o: F + KQ * o),
 )
 
 
 def gather_kernel(slots_ref, counts_ref, points_ref, factor_ref, g_ref, x_ref, *scratch):
-    mine_points, quarter, own, other, load_sem, core_sem, p_sem = scratch[:7]
-    bufs, line_sems, ring_sems, x_sems, k_sems = [scratch[7 + 4 * i : 11 + 4 * i] for i in range(5)]
+    mine_points, quarter, own, other, load_sem, core_sem = scratch[:6]
+    p_sems = scratch[6:10]
+    n = len(STREAMS)
+    bufs, line_sems, ring_sems, x_sems, k_sems = [scratch[10 + n * i : 10 + n + n * i] for i in range(5)]
     z, y, core = spot()
     x = lax.axis_index("cols")
     sibling = row_id(z, y, 1 - core)
@@ -299,14 +307,10 @@
     right, left = {"cols": (x + 1) % NX}, {"cols": (x + NX - 1) % NX}
     x_left, x_right, x_far = (x + NX - 1) % NX, (x + 1) % NX, (x + 2) % NX
 
-    def lanes(start, width):
-        return pl.ds(pl.multiple_of(start, 128), width)
-
     loads = [
         pltpu.make_async_copy(factor_ref.at[:, lanes(x * KQ, KQ)], quarter, load_sem.at[0]),
         pltpu.make_async_copy(points_ref, mine_points, load_sem.at[1]),
     ]
-    keep = pltpu.make_async_copy(points_ref, x_ref.at[:, lanes(x * FQ, FQ)], load_sem.at[2])
     for load in loads:
         load.start()
     wait_entered = enter([sibling] + y_peers + z_peers + [right, left])
@@ -335,11 +339,10 @@
     def share(index, origin, start, count, device):
         part = x_ref.at[pl.ds(start, count), lanes(origin * FQ, FQ)]
         source = points_ref if index < 2 else part
-        return remote(source, part, p_sem, index, device)
+        return remote(source, part, p_sems[index], 0, device)
 
     share(0, x, 0, ROWS, left).start()
     share(1, x, 0, ROWS, right).start()
-    keep.start()
     swap.wait()
     mine, theirs = own[...].astype(f32), other[...].astype(f32)
     first = core == 0
@@ -356,7 +359,7 @@
         here, there, peers = (z, y, y_peers) if y_first else (y, z, z_peers)
         bufs[i][here, there] = pair[:, start : start + width]
         part = bufs[i].at[here, there]
-        lines.append([remote(part, part, line_sems[i], d, peers[d]) for d in range(NY - 1)])
+        lines.append([remote(part, part, line_sems[i], 0, peers[d]) for d in range(NY - 1)])
     for d in (3, 2, 4, 1, 5, 0, 6):
         for line in lines:
             line[d].start()
@@ -384,10 +387,9 @@
     compact = (places(swapped), places(lambda position: position))
 
     for i, (start, width, y_first, _) in enumerate(STREAMS):
-        here, there, peers = (z, y, y_peers) if y_first else (y, z, z_peers)
-        for d in range(NY - 1):
-            part = bufs[i].at[here, (there + NY - 1 - d) % NY]
-            remote(part, part, line_sems[i], d, peers[d]).wait_recv()
+        here, peers = (z, y_peers) if y_first else (y, z_peers)
+        seven = bufs[i].at[here, pl.ds(0, NY - 1)]
+        remote(seven, seven, line_sems[i], 0, peers[0]).wait()
 
     def ring(buf, sems, me, count, up, down):
         last = count // 2 - 1
@@ -399,7 +401,7 @@
 
         def go_down(step, part, origin):
             piece = buf.at[origin % count, pl.ds(part * size, size)]
-            return remote(piece, piece, sems, (last + 1 + step) * PARTS + part, down)
+            return remote(piece, piece, sems, RECEIVED // 2 + step * PARTS + part - (step == last) * PARTS // 2, down)
 
         goes_up = lambda step, part: step < last or part < PARTS // 2
         goes_down = lambda step, part: step < last or part >= PARTS // 2
@@ -417,19 +419,15 @@
                 go_down(step, part, me + 1 + step).wait_recv()
 
         def finish():
-            for step in range(last + 1):
-                for part in range(PARTS):
-                    if goes_up(step, part):
-                        go_up(step, part, me + count - step).wait_send()
-                    if goes_down(step, part):
-                        go_down(step, part, me + step).wait_send()
+            sent = buf.at[pl.ds(0, count - 1)]
+            remote(sent, sent, sems, 0, up).wait_send()
 
         return send, receive, finish
 
     for i, (start, width, y_first, _) in enumerate(STREAMS):
         me, peers = (z, z_peers) if y_first else (y, y_peers)
         rings.append(ring(bufs[i], ring_sems[i], me, NZ, peers[0], peers[NZ - 2]))
-    pairs = ((0, 1), (2, 3))
+    pairs = ((0, 1),)
 
     def go(wave, step):
         for part in range(PARTS):
@@ -440,8 +438,6 @@
                     rings[i][0](step, part)
 
     half = BLOCK // 2
-    sends = []
-
     def part(i, origin, at, count=half):
         place = STREAMS[i][3](origin)
         return g_ref.at[core, pl.ds(at * half, count), lanes(place, STREAMS[i][1])]
@@ -454,11 +450,7 @@
 
     def to_sibling(i, origin, index):
         block = part(i, origin, 0, BLOCK)
-        return remote(block, block, k_sems[i], index, sibling)
-
-    def begin(copy):
-        sends.append(copy)
-        copy.start()
+        return remote(block, block, k_sems[i], 0, sibling)
 
     def join(wave):
         for i in pairs[wave]:
@@ -467,79 +459,62 @@
             placed = mm_nn(compact[int(y_first)], rows).astype(bf16)
             g_ref[core, :, lanes(STREAMS[i][3](x), width)] = placed
         for i in pairs[wave]:
-            begin(to_right(i, x, 0, 0))
-            begin(to_left(i, x, 1, 0))
+            to_right(i, x, 0, 0).start()
+            to_left(i, x, 1, 0).start()
         for i in pairs[wave]:
-            begin(to_right(i, x, 1, 1))
-            begin(to_left(i, x, 0, 1))
-            begin(to_sibling(i, x, 0))
+            to_right(i, x, 1, 1).start()
+            to_left(i, x, 0, 1).start()
+            to_sibling(i, x, 0).start()
 
     def forward(wave):
         for i in pairs[wave]:
             to_right(i, x_left, 0, 0).wait_recv()
-            begin(to_right(i, x_left, 0, 2))
+            to_right(i, x_left, 0, 2).start()
             to_left(i, x_right, 1, 0).wait_recv()
-            begin(to_left(i, x_right, 1, 2))
+            to_left(i, x_right, 1, 2).start()
 
     def collect(wave):
         for i in pairs[wave]:
             to_right(i, x_left, 1, 1).wait_recv()
-            begin(to_sibling(i, x_left, 1))
+            to_sibling(i, x_left, 1).start()
             to_left(i, x_right, 0, 1).wait_recv()
-            begin(to_sibling(i, x_right, 2))
+            to_sibling(i, x_right, 2).start()
 
     def close(wave):
         for i in pairs[wave]:
             to_right(i, x_far, 0, 2).wait_recv()
             to_left(i, x_far, 1, 2).wait_recv()
-            begin(to_sibling(i, x_far, 3))
-
-    go(0, 0)
-    go(1, 0)
-    go(0, 1)
-    go(0, 2)
-    go(1, 1)
-    share(0, x_right, 0, ROWS, left).wait_recv()
-    share(2, x_right, 0, half_rows, left).start()
-    share(1, x_left, 0, ROWS, right).wait_recv()
-    share(3, x_left, half_rows, half_rows, right).start()
-    go(0, 3)
-    go(1, 2)
-    go(0, 4)
+            to_sibling(i, x_far, 3).start()
+
+    for step in range(NZ // 2 + 1):
+        go(0, step)
+        if step == 2:
+            share(0, x_right, 0, ROWS, left).wait_recv()
+            share(2, x_right, 0, half_rows, left).start()
+            share(1, x_left, 0, ROWS, right).wait_recv()
+            share(3, x_left, half_rows, half_rows, right).start()
     join(0)
-    go(1, 3)
     forward(0)
-    go(1, 4)
-    join(1)
     collect(0)
     close(0)
-    forward(1)
-    collect(1)
-    close(1)
-    for i in range(len(STREAMS)):
-        for index, origin in enumerate((x, x_left, x_right, x_far)):
-            block = g_ref.at[1 - core, :, lanes(STREAMS[i][3](origin), STREAMS[i][1])]
-            remote(block, block, k_sems[i], index, sibling).wait_recv()
+    for i, (start, width, y_first, _) in enumerate(STREAMS):
+        rings[i][2]()
+        three = g_ref.at[core, :, lanes(0, 3 * width)]
+        remote(three, three, x_sems[i], 0, right).wait_send()
+        four = g_ref.at[core, :, lanes(0, 4 * width)]
+        remote(four, four, k_sems[i], 0, sibling).wait()
     share(2, x_far, 0, half_rows, left).wait_recv()
     share(3, x_far, half_rows, half_rows, right).wait_recv()
     share(0, x, 0, ROWS, left).wait_send()
     share(1, x, 0, ROWS, right).wait_send()
     share(2, x_right, 0, half_rows, left).wait_send()
     share(3, x_left, half_rows, half_rows, right).wait_send()
-    keep.wait()
-    for line in lines:
-        for copy in line:
-            copy.wait_send()
-    for copy in sends:
-        copy.wait_send()
-    for send, receive, finish in rings:
-        finish()
 
 
 def gather_pivots(slots, counts, points, factor):
     vmem = pl.BlockSpec(memory_space=pltpu.VMEM)
     hbm = pl.BlockSpec(memory_space=pltpu.HBM)
-    sems = lambda count: pltpu.SemaphoreType.DMA((2, count))
+    sems = lambda count: pltpu.SemaphoreType.DMA((1 + count,))
     each = len(STREAMS)
     return pl.pallas_call(
         gather_kernel,
@@ -554,14 +529,14 @@
             pltpu.VMEM((ROWS, KQ), bf16),
             pltpu.VMEM((2 * MAXP, W), bf16),
             pltpu.VMEM((2 * MAXP, W), bf16),
-            pltpu.SemaphoreType.DMA((3,)),
+            pltpu.SemaphoreType.DMA((2,)),
             sems(1),
-            sems(4),
+            *[sems(1)] * 4,
             *[pltpu.VMEM((NZ, NY, 2 * MAXP, stream[1]), bf16) for stream in STREAMS],
-            *[sems(NY - 1)] * each,
-            *[sems(NZ * PARTS)] * each,
+            *[sems(1)] * each,
+            *[sems(RECEIVED)] * each,
             *[sems(6)] * each,
-            *[sems(NX)] * each,
+            *[sems(1)] * each,
         ],
         compiler_params=pltpu.CompilerParams(
             collective_id=0, has_side_effects=True, vmem_limit_bytes=60 * 2**20
@@ -570,7 +545,9 @@
     )(slots, counts, points, factor)
 
 
-def sum_kernel(coef_ref, out_ref, got, total, got_z, piece, got_y, final, core_sem, z_sem, y_sem):
+def sum_kernel(
+    coef_ref, out_ref, got, total, rounded, got_z, piece, got_y, final, core_sem, z_sem, y_sem,
+):
     z, y, core = spot()
     sibling = row_id(z, y, 1 - core)
     z_peers = [row_id((z + d) % NZ, y, core) for d in range(1, NZ)]
@@ -582,31 +559,23 @@
     swap.start()
     swap.wait()
     total[...] = (coef_ref[core] + got[...]).reshape(NZ, 32, 128)
-    over_z = [
-        remote(total.at[(z + d + 1) % NZ], got_z.at[d], z_sem, d, z_peers[d])
-        for d in range(NZ - 1)
-    ]
-    for copy in over_z:
-        copy.start()
-    for copy in over_z:
-        copy.wait()
+    rounded[...] = total[...].astype(bf16)
+    for d in (3, 2, 4, 1, 5, 0, 6):
+        remote(rounded.at[(z + d + 1) % NZ], got_z.at[d], z_sem, 0, z_peers[d]).start()
+    remote(rounded.at[pl.ds(0, NZ - 1)], got_z, z_sem, 0, z_peers[0]).wait()
     mine = total[z]
     for d in range(NZ - 1):
-        mine = mine + got_z[d]
+        mine = mine + got_z[d].astype(f32)
     piece[...] = mine.reshape(4, 8, 128)
-    over_y = []
-    for d in range(NY):
+    for d in (4, 3, 5, 2, 6, 1, 7, 0):
         tile = piece.at[(y + d) % NY // 2]
         if d:
-            over_y.append(remote(tile, got_y.at[core, d], y_sem, d, y_same[d - 1]))
-        over_y.append(remote(tile, got_y.at[core, d], y_sem, NY + d, y_other[d]))
-    for copy in over_y:
-        copy.start()
+            remote(tile, got_y.at[core, d], y_sem, 0, y_same[d - 1]).start()
+        remote(tile, got_y.at[core, d], y_sem, 1, y_other[d]).start()
+    same, cross = got_y.at[core, pl.ds(1, NY - 1)], got_y.at[1 - core]
+    remote(same, same, y_sem, 0, y_same[0]).wait()
+    remote(cross, cross, y_sem, 1, y_other[0]).wait()
     got_y[core, 0] = piece[y // 2]
-    for d in range(NY):
-        if d:
-            remote(piece.at[0], got_y.at[core, d], y_sem, d, y_same[d - 1]).wait_recv()
-        remote(piece.at[0], got_y.at[1 - core, d], y_sem, NY + d, y_other[d]).wait_recv()
     for b in range(2):
         mine = got_y[b, 0]
         for d in range(1, NY):
@@ -615,13 +584,11 @@
     at = (y % 2) * 4 + core * 2
     out_ref[0] = final[0, pl.ds(at, 2), :]
     out_ref[1] = final[1, pl.ds(at, 2), :]
-    for copy in over_y:
-        copy.wait_send()
 
 
 def sum_coefficients(coef):
     vmem = pl.BlockSpec(memory_space=pltpu.VMEM)
-    sems = lambda count: pltpu.SemaphoreType.DMA((2, count))
+    sems = lambda count: pltpu.SemaphoreType.DMA((1 + count,))
     return pl.pallas_call(
         sum_kernel,
         in_specs=[vmem],
@@ -630,13 +597,14 @@
         scratch_shapes=[
             pltpu.VMEM((BLOCK, 128), f32),
             pltpu.VMEM((NZ, 32, 128), f32),
-            pltpu.VMEM((NZ - 1, 32, 128), f32),
+            pltpu.VMEM((NZ, 32, 128), bf16),
+            pltpu.VMEM((NZ - 1, 32, 128), bf16),
             pltpu.VMEM((4, 8, 128), f32),
             pltpu.VMEM((2, NY, 8, 128), f32),
             pltpu.VMEM((2, 8, 128), f32),
             sems(1),
-            sems(NZ - 1),
-            sems(2 * NY),
+            sems(1),
+            sems(2),
         ],
         compiler_params=pltpu.CompilerParams(collective_id=1, has_side_effects=True),
         name="coefficient_sum",
@@ -645,7 +613,7 @@
 
 def local(points, factor, targets, pivot_slots, pivot_counts):
     g, x = gather_pivots(pivot_slots, pivot_counts, points, factor)
-    new, res, coef = solve_rows(g, x, factor, targets)
+    new, res, coef = solve_rows(g, points, x, factor, targets)
     return jnp.swapaxes(new, 1, 2), res, sum_coefficients(coef)
 
 

time: 96.2 us -> 91.6 us (0.952)
  Pallas kernels: 94.1 us -> 89.5 us
    pallas_call x1, Pallas kernels: 54.9 us -> 51.5 us  [gather_pivots(): pl.pallas_call(gather_kernel, in_specs=[vmem, vmem, hbm, hbm], out_specs=...]
    pallas_call x1, Pallas kernels: 16.7 us -> 15.6 us  [sum_coefficients(): pl.pallas_call(sum_kernel, in_specs=[vmem], out_specs=vmem, out_shape=jax...]
where the time goes in v5:
time: 91.6 us; the launch traced here: 91.4 us
  Pallas kernels  89.5 us (98%)
  local copies, waits for them, and re-layouts  1.23 us (1%)
    pallas_call x1, Pallas kernels, gather_pivots(): pl.pallas_call(gather_kernel, in_specs=[vmem, vmem, hbm, hbm], out_specs=...  51.5 us
    pallas_call x1, Pallas kernels, solve_rows(): pl.pallas_call(solve_kernel, in_specs=[any_] * 5, out_specs=[vmem] * 3, o...  22.4 us
    pallas_call x1, Pallas kernels, sum_coefficients(): pl.pallas_call(sum_kernel, in_specs=[vmem], out_specs=vmem, out_shape=jax...  15.6 us

profile of v5, /device:TPU:1, one launch (start us, length us, event | category | flops | bytes accessed | tf_op | source)
XLA Modules:
  0.0 91.4 jit_solution(8194266497868014178)
XLA Ops:
  0.6 51.5 %pivot_gather.1 = (bf16[2,256,2560]{2,1,0:T(8,128)(2,1)}, bf16[1024,1024]{1,0:T(8,128)(2,1)}) custom-call(s32[2,8]{1,0:T(2,128)} %slots_ref.1, s32[2,128]{1,0:T(2,128)} %counts_ref.1, bf16[1024,256]{1,0:T(8,128)(2,1)} %p_hbm.1, bf16[1024,1536]{1,0:T(8,128)(2,1)} %f_hbm.1), custom_call_target="tpu_custom_call" | custom-call | tf_op jit(solution)/shard_map/pivot_gather/pallas_call | solution.py:519
  52.1 22.4 %pivot_solve.1 = (f32[2,64,1024]{2,1,0:T(8,128)}, f32[2,1024]{1,0:T(2,128)}, f32[2,256,128]{2,1,0:T(8,128)}) custom-call(bf16[2,256,2560]{2,1,0:T(8,128)(2,1)} %get-tuple-element.8.g_hbm, bf16[1024,256]{1,0:T(8,128)(2,1)} %p_hbm.1, bf16[1024,1024]{1,0:T(8,128)(2,1)} %get-tuple-element.9.x_hbm, bf16[1024,1536]{1,0:T(8,128)(2,1)} %f_hbm.1, bf16[1024,128]{1,0:T(8,128)(2,1)} %t_hbm.1), custom_call_target="tpu_custom_call" | custom-call | tf_op jit(solution)/shard_map/pivot_solve/pallas_call | solution.py:229
  74.6 15.6 %coefficient_sum.1 = f32[2,2,128]{2,1,0:T(2,128)} custom-call(f32[2,256,128]{2,1,0:T(8,128)} %get-tuple-element.12.coef_ref), custom_call_target="tpu_custom_call" | custom-call | tf_op jit(solution)/shard_map/coefficient_sum/pallas_call | solution.py:592
  90.2 1.2 %copy.9 = f32[2,2,128]{2,1,0:T(2,128)} copy(f32[2,2,128]{2,1,0:T(2,128)} %coefficient_sum.1) | data formatting | bytes 4096

commit v6 on v5

--- a/solution.py
+++ b/solution.py
@@ -294,11 +294,12 @@
 )
 
 
-def gather_kernel(slots_ref, counts_ref, points_ref, factor_ref, g_ref, x_ref, *scratch):
+def gather_kernel(slots_hbm, counts_hbm, points_ref, factor_ref, g_ref, x_ref, *scratch):
     mine_points, quarter, own, other, load_sem, core_sem = scratch[:6]
     p_sems = scratch[6:10]
+    slots_ref, counts_ref = scratch[10:12]
     n = len(STREAMS)
-    bufs, line_sems, ring_sems, x_sems, k_sems = [scratch[10 + n * i : 10 + n + n * i] for i in range(5)]
+    bufs, line_sems, ring_sems, x_sems, k_sems = [scratch[12 + n * i : 12 + n + n * i] for i in range(5)]
     z, y, core = spot()
     x = lax.axis_index("cols")
     sibling = row_id(z, y, 1 - core)
@@ -307,13 +308,17 @@
     right, left = {"cols": (x + 1) % NX}, {"cols": (x + NX - 1) % NX}
     x_left, x_right, x_far = (x + NX - 1) % NX, (x + 1) % NX, (x + 2) % NX
 
+    wait_entered = enter([sibling] + y_peers + z_peers + [right, left])
     loads = [
+        pltpu.make_async_copy(slots_hbm, slots_ref, load_sem.at[2]),
+        pltpu.make_async_copy(counts_hbm, counts_ref, load_sem.at[3]),
         pltpu.make_async_copy(factor_ref.at[:, lanes(x * KQ, KQ)], quarter, load_sem.at[0]),
         pltpu.make_async_copy(points_ref, mine_points, load_sem.at[1]),
     ]
     for load in loads:
         load.start()
-    wait_entered = enter([sibling] + y_peers + z_peers + [right, left])
+    for load in loads[:2]:
+        load.wait()
 
     diagonal = lax.broadcasted_iota(jnp.int32, (MAXP, MAXP), 0) == lax.broadcasted_iota(
         jnp.int32, (MAXP, MAXP), 1
@@ -326,7 +331,7 @@
     ]
     point = lax.broadcasted_iota(jnp.int32, (MAXP, ROWS), 1)
     chosen = jnp.concatenate([(point == slot).astype(f32) for slot in slots], axis=0).astype(bf16)
-    for load in loads:
+    for load in loads[2:]:
         load.wait()
     own[:, :FQ] = mm_nn(chosen, mine_points[...]).astype(bf16)
     own[:, FQ:] = mm_nn(chosen, quarter[...]).astype(bf16)
@@ -458,7 +463,6 @@
             rows = bufs[i][...].reshape(1024, width)
             placed = mm_nn(compact[int(y_first)], rows).astype(bf16)
             g_ref[core, :, lanes(STREAMS[i][3](x), width)] = placed
-        for i in pairs[wave]:
             to_right(i, x, 0, 0).start()
             to_left(i, x, 1, 0).start()
         for i in pairs[wave]:
@@ -518,7 +522,7 @@
     each = len(STREAMS)
     return pl.pallas_call(
         gather_kernel,
-        in_specs=[vmem, vmem, hbm, hbm],
+        in_specs=[hbm] * 4,
         out_specs=[vmem, hbm],
         out_shape=(
             jax.ShapeDtypeStruct((2, BLOCK, NX * W), bf16),
@@ -529,9 +533,11 @@
             pltpu.VMEM((ROWS, KQ), bf16),
             pltpu.VMEM((2 * MAXP, W), bf16),
             pltpu.VMEM((2 * MAXP, W), bf16),
-            pltpu.SemaphoreType.DMA((2,)),
+            pltpu.SemaphoreType.DMA((4,)),
             sems(1),
             *[sems(1)] * 4,
+            pltpu.VMEM((2, MAXP), jnp.int32),
+            pltpu.VMEM((2, 128), jnp.int32),
             *[pltpu.VMEM((NZ, NY, 2 * MAXP, stream[1]), bf16) for stream in STREAMS],
             *[sems(1)] * each,
             *[sems(RECEIVED)] * each,
@@ -546,19 +552,23 @@
 
 
 def sum_kernel(
-    coef_ref, out_ref, got, total, rounded, got_z, piece, got_y, final, core_sem, z_sem, y_sem,
+    coef_ref, out_ref, mine_coef, load_sem, got, total, rounded, got_z, piece, got_y, final, core_sem, z_sem, y_sem,
 ):
     z, y, core = spot()
     sibling = row_id(z, y, 1 - core)
     z_peers = [row_id((z + d) % NZ, y, core) for d in range(1, NZ)]
     y_same = [row_id(z, (y + d) % NY, core) for d in range(1, NY)]
     y_other = [row_id(z, (y + d) % NY, 1 - core) for d in range(NY)]
-    enter(z_peers + y_same + y_other)()
+    wait_entered = enter(z_peers + y_same + y_other)
+    load = pltpu.make_async_copy(coef_ref.at[core], mine_coef, load_sem)
+    load.start()
+    load.wait()
+    wait_entered()
 
     swap = remote(coef_ref.at[1 - core], got, core_sem, 0, sibling)
     swap.start()
     swap.wait()
-    total[...] = (coef_ref[core] + got[...]).reshape(NZ, 32, 128)
+    total[...] = (mine_coef[...] + got[...]).reshape(NZ, 32, 128)
     rounded[...] = total[...].astype(bf16)
     for d in (3, 2, 4, 1, 5, 0, 6):
         remote(rounded.at[(z + d + 1) % NZ], got_z.at[d], z_sem, 0, z_peers[d]).start()
@@ -591,10 +601,12 @@
     sems = lambda count: pltpu.SemaphoreType.DMA((1 + count,))
     return pl.pallas_call(
         sum_kernel,
-        in_specs=[vmem],
+        in_specs=[pl.BlockSpec(memory_space=pl.ANY)],
         out_specs=vmem,
         out_shape=jax.ShapeDtypeStruct((2, 2, 128), f32),
         scratch_shapes=[
+            pltpu.VMEM((BLOCK, 128), f32),
+            pltpu.SemaphoreType.DMA,
             pltpu.VMEM((BLOCK, 128), f32),
             pltpu.VMEM((NZ, 32, 128), f32),
             pltpu.VMEM((NZ, 32, 128), bf16),
@@ -606,7 +618,9 @@
             sems(1),
             sems(2),
         ],
-        compiler_params=pltpu.CompilerParams(collective_id=1, has_side_effects=True),
+        compiler_params=pltpu.CompilerParams(
+            collective_id=1, has_side_effects=True, vmem_limit_bytes=63 * 2**20 + 2**19
+        ),
         name="coefficient_sum",
     )(coef)
 

time: 91.6 us -> 90.4 us (0.987)
  Pallas kernels: 89.5 us -> 88.3 us
    pallas_call x2, Pallas kernels: 67.1 us -> 65.8 us  [the longest x1 50.9 us: gather_pivots(): pl.pallas_call(gather_kernel, in_specs=[hbm] * 4, out_specs=[vmem, hbm],...]
where the time goes in v6:
time: 90.4 us; the launch traced here: 90.2 us
  Pallas kernels  88.3 us (98%)
  local copies, waits for them, and re-layouts  1.23 us (1%)
    pallas_call x1, Pallas kernels, gather_pivots(): pl.pallas_call(gather_kernel, in_specs=[hbm] * 4, out_specs=[vmem, hbm],...  50.9 us
    pallas_call x1, Pallas kernels, solve_rows(): pl.pallas_call(solve_kernel, in_specs=[any_] * 5, out_specs=[vmem] * 3, o...  22.4 us
    pallas_call x1, Pallas kernels, sum_coefficients(): pl.pallas_call(sum_kernel, in_specs=[pl.BlockSpec(memory_space=pl.ANY)],...  15 us

profile of v6, /device:TPU:1, one launch (start us, length us, event | category | flops | bytes accessed | tf_op | source)
XLA Modules:
  0.0 90.2 jit_solution(2975326212877807036)
XLA Ops:
  0.6 50.9 %pivot_gather.1 = (bf16[2,256,2560]{2,1,0:T(8,128)(2,1)}, bf16[1024,1024]{1,0:T(8,128)(2,1)}) custom-call(s32[2,8]{1,0:T(2,128)} %slots_hbm.1, s32[2,128]{1,0:T(2,128)} %counts_hbm.1, bf16[1024,256]{1,0:T(8,128)(2,1)} %p_hbm.1, bf16[1024,1536]{1,0:T(8,128)(2,1)} %f_hbm.1), custom_call_target="tpu_custom_call" | custom-call | tf_op jit(solution)/shard_map/pivot_gather/pallas_call | solution.py:523
  51.5 22.4 %pivot_solve.1 = (f32[2,64,1024]{2,1,0:T(8,128)}, f32[2,1024]{1,0:T(2,128)}, f32[2,256,128]{2,1,0:T(8,128)}) custom-call(bf16[2,256,2560]{2,1,0:T(8,128)(2,1)} %get-tuple-element.8.g_hbm, bf16[1024,256]{1,0:T(8,128)(2,1)} %p_hbm.1, bf16[1024,1024]{1,0:T(8,128)(2,1)} %get-tuple-element.9.x_hbm, bf16[1024,1536]{1,0:T(8,128)(2,1)} %f_hbm.1, bf16[1024,128]{1,0:T(8,128)(2,1)} %t_hbm.1), custom_call_target="tpu_custom_call" | custom-call | tf_op jit(solution)/shard_map/pivot_solve/pallas_call | solution.py:229
  74.0 15.0 %coefficient_sum.1 = f32[2,2,128]{2,1,0:T(2,128)} custom-call(f32[2,256,128]{2,1,0:T(8,128)} %get-tuple-element.12.coef_ref), custom_call_target="tpu_custom_call" | custom-call | tf_op jit(solution)/shard_map/coefficient_sum/pallas_call | solution.py:602
  88.9 1.2 %copy.9 = f32[2,2,128]{2,1,0:T(2,128)} copy(f32[2,2,128]{2,1,0:T(2,128)} %coefficient_sum.1) | data formatting | bytes 4096

commit v7 on v6

--- a/solution.py
+++ b/solution.py
@@ -432,15 +432,13 @@
     for i, (start, width, y_first, _) in enumerate(STREAMS):
         me, peers = (z, z_peers) if y_first else (y, y_peers)
         rings.append(ring(bufs[i], ring_sems[i], me, NZ, peers[0], peers[NZ - 2]))
-    pairs = ((0, 1),)
-
-    def go(wave, step):
+
+    def go(i, step):
         for part in range(PARTS):
-            for i in pairs[wave]:
-                if step:
-                    rings[i][1](step - 1, part)
-                if step < NZ // 2:
-                    rings[i][0](step, part)
+            if step:
+                rings[i][1](step - 1, part)
+            if step < NZ // 2:
+                rings[i][0](step, part)
 
     half = BLOCK // 2
     def part(i, origin, at, count=half):
@@ -457,50 +455,50 @@
         block = part(i, origin, 0, BLOCK)
         return remote(block, block, k_sems[i], 0, sibling)
 
-    def join(wave):
-        for i in pairs[wave]:
-            width, y_first = STREAMS[i][1:3]
-            rows = bufs[i][...].reshape(1024, width)
-            placed = mm_nn(compact[int(y_first)], rows).astype(bf16)
-            g_ref[core, :, lanes(STREAMS[i][3](x), width)] = placed
-            to_right(i, x, 0, 0).start()
-            to_left(i, x, 1, 0).start()
-        for i in pairs[wave]:
-            to_right(i, x, 1, 1).start()
-            to_left(i, x, 0, 1).start()
-            to_sibling(i, x, 0).start()
-
-    def forward(wave):
-        for i in pairs[wave]:
+    def join(i):
+        width, y_first = STREAMS[i][1:3]
+        rows = bufs[i][...].reshape(1024, width)
+        placed = mm_nn(compact[int(y_first)], rows).astype(bf16)
+        g_ref[core, :, lanes(STREAMS[i][3](x), width)] = placed
+        to_right(i, x, 0, 0).start()
+        to_left(i, x, 1, 0).start()
+        to_right(i, x, 1, 1).start()
+        to_left(i, x, 0, 1).start()
+        to_sibling(i, x, 0).start()
+
+    def forward():
+        for i in range(len(STREAMS)):
             to_right(i, x_left, 0, 0).wait_recv()
             to_right(i, x_left, 0, 2).start()
             to_left(i, x_right, 1, 0).wait_recv()
             to_left(i, x_right, 1, 2).start()
 
-    def collect(wave):
-        for i in pairs[wave]:
+    def collect():
+        for i in range(len(STREAMS)):
             to_right(i, x_left, 1, 1).wait_recv()
             to_sibling(i, x_left, 1).start()
             to_left(i, x_right, 0, 1).wait_recv()
             to_sibling(i, x_right, 2).start()
 
-    def close(wave):
-        for i in pairs[wave]:
+    def close():
+        for i in range(len(STREAMS)):
             to_right(i, x_far, 0, 2).wait_recv()
             to_left(i, x_far, 1, 2).wait_recv()
             to_sibling(i, x_far, 3).start()
 
     for step in range(NZ // 2 + 1):
-        go(0, step)
+        for i in range(len(STREAMS)):
+            go(i, step)
+            if step == NZ // 2:
+                join(i)
         if step == 2:
             share(0, x_right, 0, ROWS, left).wait_recv()
             share(2, x_right, 0, half_rows, left).start()
             share(1, x_left, 0, ROWS, right).wait_recv()
             share(3, x_left, half_rows, half_rows, right).start()
-    join(0)
-    forward(0)
-    collect(0)
-    close(0)
+    forward()
+    collect()
+    close()
     for i, (start, width, y_first, _) in enumerate(STREAMS):
         rings[i][2]()
         three = g_ref.at[core, :, lanes(0, 3 * width)]

time: 90.4 us -> 91.3 us (level)
  no operation moved by 1% of the time
where the time goes in v7:
time: 91.3 us; the launch traced here: 91.1 us
  Pallas kernels  89.2 us (98%)
  local copies, waits for them, and re-layouts  1.23 us (1%)
    pallas_call x1, Pallas kernels, gather_pivots(): pl.pallas_call(gather_kernel, in_specs=[hbm] * 4, out_specs=[vmem, hbm],...  51.8 us
    pallas_call x1, Pallas kernels, solve_rows(): pl.pallas_call(solve_kernel, in_specs=[any_] * 5, out_specs=[vmem] * 3, o...  22.4 us
    pallas_call x1, Pallas kernels, sum_coefficients(): pl.pallas_call(sum_kernel, in_specs=[pl.BlockSpec(memory_space=pl.ANY)],...  15 us

profile of v7, /device:TPU:1, one launch (start us, length us, event | category | flops | bytes accessed | tf_op | source)
XLA Modules:
  0.0 91.1 jit_solution(2948989517555097995)
XLA Ops:
  0.6 51.8 %pivot_gather.1 = (bf16[2,256,2560]{2,1,0:T(8,128)(2,1)}, bf16[1024,1024]{1,0:T(8,128)(2,1)}) custom-call(s32[2,8]{1,0:T(2,128)} %slots_hbm.1, s32[2,128]{1,0:T(2,128)} %counts_hbm.1, bf16[1024,256]{1,0:T(8,128)(2,1)} %p_hbm.1, bf16[1024,1536]{1,0:T(8,128)(2,1)} %f_hbm.1), custom_call_target="tpu_custom_call" | custom-call | tf_op jit(solution)/shard_map/pivot_gather/pallas_call | solution.py:521
  52.4 22.4 %pivot_solve.1 = (f32[2,64,1024]{2,1,0:T(8,128)}, f32[2,1024]{1,0:T(2,128)}, f32[2,256,128]{2,1,0:T(8,128)}) custom-call(bf16[2,256,2560]{2,1,0:T(8,128)(2,1)} %get-tuple-element.8.g_hbm, bf16[1024,256]{1,0:T(8,128)(2,1)} %p_hbm.1, bf16[1024,1024]{1,0:T(8,128)(2,1)} %get-tuple-element.9.x_hbm, bf16[1024,1536]{1,0:T(8,128)(2,1)} %f_hbm.1, bf16[1024,128]{1,0:T(8,128)(2,1)} %t_hbm.1), custom_call_target="tpu_custom_call" | custom-call | tf_op jit(solution)/shard_map/pivot_solve/pallas_call | solution.py:229
  74.8 15.0 %coefficient_sum.1 = f32[2,2,128]{2,1,0:T(2,128)} custom-call(f32[2,256,128]{2,1,0:T(8,128)} %get-tuple-element.12.coef_ref), custom_call_target="tpu_custom_call" | custom-call | tf_op jit(solution)/shard_map/coefficient_sum/pallas_call | solution.py:600
  89.8 1.2 %copy.9 = f32[2,2,128]{2,1,0:T(2,128)} copy(f32[2,2,128]{2,1,0:T(2,128)} %coefficient_sum.1) | data formatting | bytes 4096
